TPU v7x, 128 devices: a whole 4x4x4 slice. The times are simulated.
128 devices in a mesh: dp: 32 (over x, y, z_lo), mp: 4 (over z_hi, core).
Axes of the slice: x: 4, y: 4, z: 4 (z_hi: 2, z_lo: 2; z = z_hi * 2 + z_lo), core: 2. Of those that a mesh axis runs over, the one named last changes fastest.
Arguments:
- activations: bfloat16 [16384, 8192], P('dp', 'mp'), may hold values from -6 to 6
- out_grads: bfloat16 [16384, 1024], P('dp'), may hold values from -0.06591797 to 0.06591797
- projector: bfloat16 [8192, 512], P('mp'), may hold values from -0.0625 to 0.0625
- weight: float32 [8192, 1024], P('mp'), may hold values from -0.00024 to 0.00024
- first_moment: float32 [512, 1024], P('dp', 'mp'), may hold values from -0.6 to 0.6
- second_moment: float32 [512, 1024], P('dp', 'mp'), may hold values from 0.0003 to 0.003
Outputs:
- new_weight: float32 [8192, 1024], P('mp')
- update: bfloat16 [8192, 1024], P('mp')
- first_new: float32 [512, 1024], P('dp', 'mp')
- second_new: float32 [512, 1024], P('dp', 'mp')
All inputs are finite; a program needn't handle non-finite values.
Results may differ from a plain program's by a relative error of at most 0.008.
Values may be sent and summed in bfloat16 or wider, within the bound.
A program may use at most 128 MiB of HBM per device.

v0:
```python
import jax
import jax.numpy as jnp
from jax import lax
from jax.sharding import PartitionSpec as P

first_decay = 0.9
second_decay = 0.999
first_bias = 1.0 - 0.9**2
second_bias = 1.0 - 0.999**2
epsilon = 1e-08
step_rate = 0.00025


def split_up(x, dim, length):
    before, after = (x.shape[:dim], x.shape[dim + 1 :])
    return jnp.moveaxis(x.reshape(*before, length, -1, *after), dim, 0)


def sum_at_owner(x, axis, dim):
    length = lax.axis_size(axis)
    parts = lax.all_to_all(split_up(x, dim, length), axis, 0, 0, tiled=True)
    return jnp.sum(parts.astype(jnp.float32), axis=0)


def sent_and_summed(x, axis, dim):
    parts = split_up(x, dim, lax.axis_size(axis))
    arrived = lax.all_to_all(parts, axis, split_axis=0, concat_axis=0, tiled=True)
    return arrived.sum(axis=0)


def in_order(parts, dim):
    parts = jnp.moveaxis(parts, 0, dim)
    shape = parts.shape
    return parts.reshape(*shape[:dim], shape[dim] * shape[dim + 1], *shape[dim + 2 :])


def sent_to_all(x, axis):
    length = lax.axis_size(axis)
    return lax.all_to_all(jnp.broadcast_to(x[None], (length, *x.shape)), axis, 0, 0, tiled=True)


def collect(x, axis, dim):
    return in_order(sent_to_all(x, axis), dim)


def local(activations, out_grads, projector, weight, first_moment, second_moment):
    projected = jnp.dot(activations, projector, preferred_element_type=jnp.float32)
    partial_value = lax.dot_general(
        projected,
        out_grads.astype(jnp.float32),
        (((0,), (0,)), ((), ())),
        precision=lax.Precision.HIGHEST,
    )
    rank_block = sum_at_owner(partial_value.astype(jnp.bfloat16), "dp", 0)
    coefficients = sent_and_summed(rank_block, "mp", 1)
    first_new = first_decay * first_moment + (1.0 - first_decay) * coefficients
    second_new = second_decay * second_moment + (1.0 - second_decay) * coefficients * coefficients
    normalized = (first_new / first_bias / (jnp.sqrt(second_new / second_bias) + epsilon)).astype(
        jnp.bfloat16
    )
    tall_block = collect(normalized, "dp", 0)
    expanded = jnp.dot(projector, collect(tall_block, "mp", 1), preferred_element_type=jnp.float32)
    new_weight = weight - step_rate * expanded
    return (new_weight, expanded.astype(jnp.bfloat16), first_new, second_new)


def solution(mesh):
    in_specs = (
        P("dp", "mp"),
        P("dp", None),
        P("mp", None),
        P("mp", None),
        P("dp", "mp"),
        P("dp", "mp"),
    )
    out_specs = (P("mp", None), P("mp", None), P("dp", "mp"), P("dp", "mp"))
    return jax.shard_map(local, mesh=mesh, in_specs=in_specs, out_specs=out_specs, check_vma=False)
```

profile of v0, /device:TPU:1, one launch (start us, length us, event | category | flops | bytes accessed | tf_op | source)
XLA Modules:
  0.0 104.0 jit_solution(15705517898818759692)
XLA Ops:
  0.6 0.0 copy-start
  0.6 0.0 copy-start.1
  0.7 1.6 %copy-done = bf16[2048,512]{1,0:T(8,128)(2,1)S(1)} copy-done((bf16[2048,512]{1,0:T(8,128)(2,1)S(1)}, bf16[2048,512]{1,0:T(8,128)(2,1)}, u32[]{:S(2)}) %copy-start) | copy-done | bytes 2097176
  2.2 2.8 %fusion.2 = f32[512,512]{1,0:T(8,128)S(1)} fusion(bf16[512,2048]{1,0:T(8,128)(2,1)} %param.6, bf16[2048,512]{1,0:T(8,128)(2,1)S(1)} %copy-done), kind=kOutput, calls=%fused_computation.8 | convolution fusion | flops 1073741824 | bytes 5242880 | tf_op jit(solution)/shard_map/dot_general | solution.py:47
  5.1 0.0 copy-done.1
  5.1 1.8 %convolution_convert_fusion = bf16[512,1024]{1,0:T(8,128)(2,1)S(1)} fusion(f32[512,512]{1,0:T(8,128)S(1)} %fusion.2, bf16[512,1024]{1,0:T(8,128)(2,1)S(1)} %copy-done.1), kind=kOutput, calls=%fused_computation.3 | convolution fusion | flops 3221749760 | bytes 3145728 | tf_op jit(solution)/shard_map/dot_general | solution.py:48
  6.9 0.0 copy-start.2
  6.9 0.0 copy-start.3
  7.0 25.3 %all_to_all.20 = bf16[32,16,1024]{2,1,0:T(8,128)(2,1)S(1)} all-to-all(bf16[32,16,1024]{2,1,0:T(8,128)(2,1)S(1)} %bitcast.19), channel_id=1, replica_groups=mesh['dp'=32,'mp'=4] {'dp'}, dimensions={0} | all-to-all | bytes 2097152 | tf_op jit(solution)/shard_map/all_to_all | solution.py:21
  32.2 0.2 convert_reduce_fusion
  32.4 11.6 %all_to_all.21 = f32[4,16,256]{2,1,0:T(8,128)S(1)} all-to-all(f32[4,16,256]{2,1,0:T(8,128)S(1)} %copy.25), channel_id=1, replica_groups=mesh['dp'=32,'mp'=4] {'mp'}, dimensions={0} | all-to-all | bytes 131072 | tf_op jit(solution)/shard_map/all_to_all | solution.py:27
  44.1 0.0 copy-done.2
  44.1 0.0 copy-done.3
  44.1 0.6 divide_convert_fusion
  44.7 11.5 %all_to_all.22 = bf16[32,16,256]{2,1,0:T(8,128)(2,1)S(1)} all-to-all(bf16[32,16,256]{2,1,0:T(8,128)(2,1)S(1)} %broadcast_in_dim.6), channel_id=1, replica_groups=mesh['dp'=32,'mp'=4] {'dp'}, dimensions={0} | all-to-all | bytes 524288 | tf_op jit(solution)/shard_map/all_to_all | solution.py:39
  56.2 0.1 copy.26
  56.3 1.1 %broadcast_in_dim.15 = bf16[4,512,256]{1,2,0:T(8,128)(2,1)} broadcast(bf16[512,256]{0,1:T(8,128)(2,1)S(1)} %copy.26), dimensions={1,2} | broadcast | bytes 1310720 | tf_op jit(solution)/shard_map/broadcast_in_dim | solution.py:39
  57.4 5.7 %all-to-all-start.3 = ((bf16[4,512,256]{1,2,0:T(8,128)(2,1)}), bf16[4,512,256]{1,2,0:T(8,128)(2,1)S(1)}, u32[]{:S(2)}, u32[]{:S(2)}) async-start(bf16[4,512,256]{1,2,0:T(8,128)(2,1)} %broadcast_in_dim.15), calls=%async_computation.3 | async-start | bytes 2097152 | tf_op jit(solution)/shard_map/all_to_all | solution.py:39
  63.1 9.1 %copy.27 = f32[2048,1024]{0,1:T(8,128)} copy(f32[2048,1024]{1,0:T(8,128)} %param.9) | data formatting | bytes 16777216 | tf_op args[3]
  72.2 6.0 %all-to-all-done.3 = bf16[4,512,256]{1,2,0:T(8,128)(2,1)S(1)} async-done(((bf16[4,512,256]{1,2,0:T(8,128)(2,1)}), bf16[4,512,256]{1,2,0:T(8,128)(2,1)S(1)}, u32[]{:S(2)}, u32[]{:S(2)}) %all-to-all-start.3) | async-done | bytes 1048608 | tf_op jit(solution)/shard_map/all_to_all | solution.py:39
  78.2 10.2 %bitcast_subtract_fusion = (f32[2048,1024]{0,1:T(8,128)}, bf16[1024,2048]{1,0:T(8,128)(2,1)}) fusion(f32[2048,1024]{0,1:T(8,128)} %copy.27, bf16[512,1024]{0,1:T(8,128)(2,1)S(1)} %bitcast.18, bf16[2048,512]{1,0:T(8,128)(2,1)S(1)} %copy-done), kind=kOutput, calls=%fused_computation | convolution fusion | flops 2153775104 | bytes 24117248 | tf_op jit(solution)/shard_map/dot_general | solution.py:62
  88.4 9.2 %copy.28 = f32[2048,1024]{1,0:T(8,128)} copy(f32[2048,1024]{0,1:T(8,128)} %get-tuple-element.27) | data formatting | bytes 16777216
  97.6 6.4 %copy.29 = bf16[2048,1024]{1,0:T(8,128)(2,1)} copy(bf16[2048,1024]{0,1:T(8,128)(2,1)} %bitcast.17) | data formatting | bytes 8388608
  (4 shorter events, 0.1 us)
Async XLA Ops:
  0.6 1.6 %copy-start = (bf16[2048,512]{1,0:T(8,128)(2,1)S(1)}, bf16[2048,512]{1,0:T(8,128)(2,1)}, u32[]{:S(2)}) copy-start(bf16[2048,512]{1,0:T(8,128)(2,1)} %param.8) | copy-start | bytes 6291460
  0.6 4.4 %copy-start.1 = (bf16[512,1024]{1,0:T(8,128)(2,1)S(1)}, bf16[512,1024]{1,0:T(8,128)(2,1)}, u32[]{:S(2)}) copy-start(bf16[512,1024]{1,0:T(8,128)(2,1)} %param.7) | copy-start | bytes 3145732
  6.9 37.1 %copy-start.2 = (f32[16,256]{1,0:T(8,128)S(1)}, f32[16,256]{1,0:T(8,128)}, u32[]{:S(2)}) copy-start(f32[16,256]{1,0:T(8,128)} %param.10) | copy-start | bytes 49156
  6.9 37.1 %copy-start.3 = (f32[16,256]{1,0:T(8,128)S(1)}, f32[16,256]{1,0:T(8,128)}, u32[]{:S(2)}) copy-start(f32[16,256]{1,0:T(8,128)} %param.11) | copy-start | bytes 49156
  57.4 20.8 %all-to-all-start.3 = ((bf16[4,512,256]{1,2,0:T(8,128)(2,1)}), bf16[4,512,256]{1,2,0:T(8,128)(2,1)S(1)}, u32[]{:S(2)}, u32[]{:S(2)}) async-start(bf16[4,512,256]{1,2,0:T(8,128)(2,1)} %broadcast_in_dim.15), calls=%async_computation.3 | async-start | bytes 2097152 | tf_op jit(solution)/shard_map/all_to_all | solution.py:39
where the time goes:
time: 105 us; the launch traced here: 104 us
  blocking collectives  48.3 us (46%)
  local copies, waits for them, and re-layouts  27.6 us (26%)
  matrix products  14.9 us (14%)
  waiting for transfers between devices  5.98 us (6%)
  starting transfers between devices  5.67 us (5%)
    unnamed x11, local copies, waits for them, and re-layouts  26.4 us
    all_to_all x1, blocking collectives, sum_at_owner(): parts = lax.all_to_all(split_up(x, dim, length), axis, 0, 0, tiled=True)  25.3 us
    all_to_all x1, blocking collectives, sent_and_summed(): lax.all_to_all(parts, axis, split_axis=0, concat_axis=0, tiled=True)  11.6 us
    all_to_all x1, blocking collectives, sent_to_all(): lax.all_to_all(jnp.broadcast_to(x[None], (length, *x.shape)), axis, 0, 0,...  11.5 us
    dot_general x1, matrix products, local(): jnp.dot(projector, collect(tall_block, 'mp', 1), preferred_element_type=j...  10.2 us
    all_to_all x1, waiting for transfers between devices, sent_to_all(): lax.all_to_all(jnp.broadcast_to(x[None], (length, *x.shape)), axis, 0, 0,...  5.98 us
    all_to_all x1, starting transfers between devices, sent_to_all(): lax.all_to_all(jnp.broadcast_to(x[None], (length, *x.shape)), axis, 0, 0,...  5.67 us
    dot_general x1, matrix products, local(): jnp.dot(activations, projector, preferred_element_type=jnp.float32)  2.84 us
  transfers between devices with their start and end apart: 1, of which 1 were waited for; matrix products, arithmetic and copies ran while one was open for 9% of the time, Pallas kernels for 0%

commit v1 on v0

v1 whole, which is shorter than its diff:
```python
import functools

import jax
import jax.numpy as jnp
from jax import lax
from jax.experimental import pallas as pl
from jax.experimental.pallas import tpu as pltpu
from jax.sharding import PartitionSpec as P

first_decay = 0.9
second_decay = 0.999
first_bias = 1.0 - 0.9**2
second_bias = 1.0 - 0.999**2
epsilon = 1e-08
step_rate = 0.00025

MESH = pl.DeviceIdType.MESH
F32 = jnp.float32
BF16 = jnp.bfloat16
TOKEN_CHUNKS = 4


def reduce_kernel(
    acts,
    grads,
    proj,
    first_moment,
    second_moment,
    gathered,
    first_new_ref,
    second_new_ref,
    acts_v,
    proj_v,
    grads_v,
    mine,
    theirs,
    summed,
    parts,
    got1,
    sums1,
    got2,
    sums2,
    got3,
    load_sem,
    pair_send,
    pair_recv,
    rs_send,
    rs_recv,
    ag_send,
    ag_recv,
    fw_send,
    fw_recv,
):
    dp = lax.axis_index("dp")
    mp = lax.axis_index("mp")
    x, y, zl = dp // 8, (dp // 2) % 4, dp % 2
    zh, c = mp // 2, mp % 2
    z = zh * 2 + zl

    def at_x(d):
        return (((x + d) % 4) * 8 + y * 2 + zl, mp)

    def at_y(d):
        return (x * 8 + ((y + d) % 4) * 2 + zl, mp)

    def at_z(d):
        to = (z + d) % 4
        return (x * 8 + y * 2 + to % 2, (to // 2) * 2 + c)

    sibling = (dp, zh * 2 + 1 - c)

    tokens = acts.shape[0]
    chunk = tokens // TOKEN_CHUNKS
    load_proj = pltpu.make_async_copy(proj, proj_v, load_sem.at[0])
    load_proj.start()
    load_acts = []
    for t in range(TOKEN_CHUNKS):
        rows = pl.ds(t * chunk, chunk)
        copy = pltpu.make_async_copy(acts.at[rows], acts_v.at[rows], load_sem.at[1 + t])
        copy.start()
        load_acts.append(copy)
    load_grads = []
    for h in range(2):
        columns = pl.ds(pl.multiple_of(h * 512 + c * 256, 256), 256)
        copy = pltpu.make_async_copy(
            grads.at[:, columns], grads_v.at[:, pl.ds(h * 256, 256)], load_sem.at[1 + TOKEN_CHUNKS + h]
        )
        copy.start()
        load_grads.append(copy)

    barrier = pltpu.get_barrier_semaphore()
    for partner in [sibling] + [at(d) for at in (at_x, at_y, at_z) for d in (1, 2, 3)]:
        pl.semaphore_signal(barrier, inc=1, device_id=partner, device_id_type=MESH)

    def remote(src, dst, send, recv, device):
        return pltpu.make_async_remote_copy(
            src_ref=src, dst_ref=dst, send_sem=send, recv_sem=recv, device_id=device, device_id_type=MESH
        )

    load_proj.wait()
    pair = []
    for t in range(TOKEN_CHUNKS):
        rows = pl.ds(t * chunk, chunk)
        load_acts[t].wait()
        projected = jnp.dot(acts_v[rows, :], proj_v[...], preferred_element_type=F32)
        mine[rows, :] = projected.astype(BF16)
        summed[rows, :] = projected
        if t == 0:
            pl.semaphore_wait(barrier, 10)
        copy = remote(mine.at[rows], theirs.at[rows], pair_send.at[t], pair_recv.at[t], sibling)
        copy.start()
        pair.append(copy)
    for copy in load_grads:
        copy.wait()
    for t in range(TOKEN_CHUNKS):
        rows = pl.ds(t * chunk, chunk)
        pair[t].wait()
        mine[rows, :] = (summed[rows, :] + theirs[rows, :].astype(F32)).astype(BF16)

    started = []
    for b in range(4):
        block = lax.dot_general(
            mine[:, b * 128 : (b + 1) * 128],
            grads_v[...],
            (((0,), (0,)), ((), ())),
            preferred_element_type=F32,
        ).astype(BF16)
        for h in range(2):
            for half in range(2):
                first = h * 256 + half * 128
                parts[h, half, b] = block[:, first : first + 128].reshape(4, 32, 128)

    stage = []
    for d in (2, 1, 3):
        a = remote(
            parts.at[:, 0, (x + d) % 4], got1.at[0, d - 1], rs_send.at[0, 0, d - 1], rs_recv.at[0, 0, d - 1], at_x(d)
        )
        b = remote(
            parts.at[:, 1, :, (y + d) % 4], got1.at[1, d - 1], rs_send.at[0, 1, d - 1], rs_recv.at[0, 1, d - 1], at_y(d)
        )
        a.start()
        b.start()
        stage.append((a, b))
    started += [copy for both in stage for copy in both]
    for half in range(2):
        for both in stage:
            both[half].wait_recv()
        own = parts[:, 0, x] if half == 0 else parts[:, 1, :, y]
        total = own.astype(F32)
        for s in range(3):
            total += got1[half, s].astype(F32)
        sums1[half] = total.astype(BF16)
        again = []
        for d in (2, 1, 3):
            to, device = ((y + d) % 4, at_y(d)) if half == 0 else ((x + d) % 4, at_x(d))
            copy = remote(
                sums1.at[half, :, to],
                got2.at[half, d - 1],
                rs_send.at[1, half, d - 1],
                rs_recv.at[1, half, d - 1],
                device,
            )
            copy.start()
            again.append(copy)
        started += again
        if half == 0:
            second = [again]
        else:
            second.append(again)
    for half in range(2):
        for copy in second[half]:
            copy.wait_recv()
        own = sums1[half, :, y] if half == 0 else sums1[half, :, x]
        total = own.astype(F32)
        for s in range(3):
            total += got2[half, s].astype(F32)
        sums2[:, :, :, half * 128 : (half + 1) * 128] = total.reshape(2, 2, 16, 128)
    third = []
    for d in (2, 1, 3):
        to = (z + d) % 4
        copy = remote(
            sums2.at[to // 2, to % 2], got3.at[d - 1], rs_send.at[2, 0, d - 1], rs_recv.at[2, 0, d - 1], at_z(d)
        )
        copy.start()
        third.append(copy)
    started += third
    for copy in third:
        copy.wait_recv()
    coefficients = sums2[zh, zl] + got3[0] + got3[1] + got3[2]

    first_new = first_decay * first_moment[...] + (1.0 - first_decay) * coefficients
    second_new = second_decay * second_moment[...] + (1.0 - second_decay) * coefficients * coefficients
    first_new_ref[...] = first_new
    second_new_ref[...] = second_new
    normalized = first_new / first_bias / (jnp.sqrt(second_new / second_bias) + epsilon)
    normalized = normalized.astype(BF16)
    gathered[zh, c, 0, x, y, zl] = normalized[:, :128]
    gathered[zh, c, 1, x, y, zl] = normalized[:, 128:]

    def spread(src, send, recv, device):
        copy = remote(src, src, send, recv, device)
        copy.start()
        started.append(copy)
        return copy

    forwards = []

    def forward(src, n):
        forwards.append(spread(src, fw_send.at[n], fw_recv.at[n], sibling))

    ring = [
        (spread(gathered.at[zh, c, :, x, y, zl], ag_send.at[0, 0, d - 1], ag_recv.at[0, 0, d - 1], at_z(d)), d)
        for d in (2, 1, 3)
    ]
    for copy, d in ring:
        copy.wait_recv()
    ring_a, ring_b = [], []
    for d in (2, 1, 3):
        ring_a.append(
            (spread(gathered.at[:, c, 0, x, y], ag_send.at[1, 0, d - 1], ag_recv.at[1, 0, d - 1], at_y(d)), d)
        )
        ring_b.append(
            (spread(gathered.at[:, c, 1, x, y], ag_send.at[1, 1, d - 1], ag_recv.at[1, 1, d - 1], at_x(d)), d)
        )
    forward(gathered.at[:, c, :, x, y], 0)
    for copy, d in ring_a:
        copy.wait_recv()
    last_a, last_b = [], []
    for d in (2, 1, 3):
        last_a.append((spread(gathered.at[:, c, 0, x], ag_send.at[2, 0, d - 1], ag_recv.at[2, 0, d - 1], at_x(d)), d))
    for copy, d in ring_b:
        copy.wait_recv()
    for d in (2, 1, 3):
        last_b.append(
            (spread(gathered.at[:, c, 1, :, y], ag_send.at[2, 1, d - 1], ag_recv.at[2, 1, d - 1], at_y(d)), d)
        )
    for copy, d in ring_a:
        forward(gathered.at[:, c, 0, x, (y - d + 4) % 4], d)
    for copy, d in ring_b:
        forward(gathered.at[:, c, 1, (x - d + 4) % 4, y], 3 + d)
    for n in (1, 2, 0):
        copy, d = last_a[n]
        copy.wait_recv()
        forward(gathered.at[:, c, 0, (x - d + 4) % 4], 6 + d)
        copy, d = last_b[n]
        copy.wait_recv()
        forward(gathered.at[:, c, 1, :, (y - d + 4) % 4], 9 + d)
    for copy in forwards:
        copy.wait_recv()
    for copy in started:
        copy.wait_send()


def reduce_and_gather(acts, grads, proj, first_moment, second_moment):
    vmem = pl.BlockSpec(memory_space=pltpu.VMEM)
    hbm = pl.BlockSpec(memory_space=pl.ANY)
    dma = pltpu.SemaphoreType.DMA
    return pl.pallas_call(
        reduce_kernel,
        out_shape=(
            jax.ShapeDtypeStruct((2, 2, 2, 4, 4, 2, 16, 128), BF16),
            jax.ShapeDtypeStruct((16, 256), F32),
            jax.ShapeDtypeStruct((16, 256), F32),
        ),
        in_specs=[hbm, hbm, hbm, vmem, vmem],
        out_specs=(vmem, vmem, vmem),
        scratch_shapes=[
            pltpu.VMEM((512, 2048), BF16),
            pltpu.VMEM((2048, 512), BF16),
            pltpu.VMEM((512, 512), BF16),
            pltpu.VMEM((512, 512), BF16),
            pltpu.VMEM((512, 512), BF16),
            pltpu.VMEM((512, 512), F32),
            pltpu.VMEM((2, 2, 4, 4, 32, 128), BF16),
            pltpu.VMEM((2, 3, 2, 4, 32, 128), BF16),
            pltpu.VMEM((2, 2, 4, 32, 128), BF16),
            pltpu.VMEM((2, 3, 2, 32, 128), BF16),
            pltpu.VMEM((2, 2, 16, 256), F32),
            pltpu.VMEM((3, 16, 256), F32),
            dma((3 + TOKEN_CHUNKS,)),
            dma((TOKEN_CHUNKS,)),
            dma((TOKEN_CHUNKS,)),
            dma((3, 2, 3)),
            dma((3, 2, 3)),
            dma((3, 2, 3)),
            dma((3, 2, 3)),
            dma((13,)),
            dma((13,)),
        ],
        compiler_params=pltpu.CompilerParams(
            collective_id=0, has_side_effects=True, vmem_limit_bytes=24 * 1024 * 1024
        ),
    )(acts, grads, proj, first_moment, second_moment)


def expand_kernel(gathered, proj, weight, first_in, second_in, new_weight, update, first_out, second_out):
    @pl.when(pl.program_id(0) == 0)
    def _():
        first_out[...] = first_in[...]
        second_out[...] = second_in[...]

    rows = proj[...]
    for n in range(4):
        columns = slice(n * 256, (n + 1) * 256)
        block = jnp.concatenate([gathered[2 * n], gathered[2 * n + 1]], axis=1)
        expanded = jnp.dot(rows, block, preferred_element_type=F32)
        new_weight[:, columns] = weight[:, columns] - step_rate * expanded
        update[:, columns] = expanded.astype(BF16)


def expand(gathered, proj, weight, first_new, second_new):
    depth, rank = proj.shape
    tile = 256
    whole = lambda *shape: pl.BlockSpec(shape, lambda i: (0,) * len(shape))
    return pl.pallas_call(
        expand_kernel,
        grid=(depth // tile,),
        out_shape=(
            jax.ShapeDtypeStruct((depth, 1024), F32),
            jax.ShapeDtypeStruct((depth, 1024), BF16),
            jax.ShapeDtypeStruct((16, 256), F32),
            jax.ShapeDtypeStruct((16, 256), F32),
        ),
        in_specs=[
            whole(8, rank, 128),
            pl.BlockSpec((tile, rank), lambda i: (i, 0)),
            pl.BlockSpec((tile, 1024), lambda i: (i, 0)),
            whole(16, 256),
            whole(16, 256),
        ],
        out_specs=(
            pl.BlockSpec((tile, 1024), lambda i: (i, 0)),
            pl.BlockSpec((tile, 1024), lambda i: (i, 0)),
            whole(16, 256),
            whole(16, 256),
        ),
        compiler_params=pltpu.CompilerParams(vmem_limit_bytes=16 * 1024 * 1024),
    )(gathered, proj, weight, first_new, second_new)


def local(activations, out_grads, projector, weight, first_moment, second_moment):
    gathered, first_new, second_new = reduce_and_gather(
        activations, out_grads, projector, first_moment, second_moment
    )
    gathered = gathered.reshape(8, 512, 128)
    return tuple(expand(gathered, projector, weight, first_new, second_new))


def solution(mesh):
    in_specs = (
        P("dp", "mp"),
        P("dp", None),
        P("mp", None),
        P("mp", None),
        P("dp", "mp"),
        P("dp", "mp"),
    )
    out_specs = (P("mp", None), P("mp", None), P("dp", "mp"), P("dp", "mp"))
    return jax.shard_map(local, mesh=mesh, in_specs=in_specs, out_specs=out_specs, check_vma=False)
```

time: 105 us -> 55.6 us (0.53)
  blocking collectives: 48.3 us -> 0 us
  Pallas kernels: 0 us -> 45.3 us
  local copies, waits for them, and re-layouts: 27.6 us -> 9.21 us
  matrix products: 14.9 us -> 0 us
  waiting for transfers between devices: 5.98 us -> 0 us
  starting transfers between devices: 5.67 us -> 0 us
    all_to_all x3 -> x0, blocking collectives: 48.3 us -> none  [the longest x1 25.3 us: sum_at_owner(): parts = lax.all_to_all(split_up(x, dim, length), axis, 0, 0, tiled=True)]
    pallas_call x0 -> x2, Pallas kernels: none -> 45.3 us  [the longest x1 38.5 us: reduce_and_gather(): pl.pallas_call(reduce_kernel, out_shape=(jax.ShapeDtypeStruct((2, 2, 2, 4...]
    unnamed x11 -> x14, local copies, waits for them, and re-layouts: 26.4 us -> 9.21 us
    dot_general x3 -> x0, matrix products: 14.9 us -> none  [the longest x1 10.2 us: local(): jnp.dot(projector, collect(tall_block, 'mp', 1), preferred_element_type=j...]
    all_to_all x1 -> x0, waiting for transfers between devices: 5.98 us -> none  [sent_to_all(): lax.all_to_all(jnp.broadcast_to(x[None], (length, *x.shape)), axis, 0, 0,...]
    all_to_all x1 -> x0, starting transfers between devices: 5.67 us -> none  [sent_to_all(): lax.all_to_all(jnp.broadcast_to(x[None], (length, *x.shape)), axis, 0, 0,...]
    broadcast_in_dim x3 -> x0, local copies, waits for them, and re-layouts: 1.21 us -> none  [sent_to_all(): jnp.broadcast_to(x[None], (length, *x.shape))]
  transfers between devices with their start and end apart: 1 -> 0, of which waited for: 1 -> 0; matrix products, arithmetic and copies ran while one was open for 9% -> 0% of each run, Pallas kernels for 0% -> 0%
where the time goes in v1:
time: 55.6 us; the launch traced here: 55.2 us
  Pallas kernels  45.3 us (81%)
  local copies, waits for them, and re-layouts  9.21 us (17%)
  between operations  0.67 us (1%)
    pallas_call x1, Pallas kernels, reduce_and_gather(): pl.pallas_call(reduce_kernel, out_shape=(jax.ShapeDtypeStruct((2, 2, 2, 4...  38.5 us
    unnamed x14, local copies, waits for them, and re-layouts  9.21 us
    pallas_call x1, Pallas kernels, expand(): pl.pallas_call(expand_kernel, grid=(depth // tile,), out_shape=(jax.Shape...  6.82 us

profile of v1, /device:TPU:1, one launch (start us, length us, event | category | flops | bytes accessed | tf_op | source)
XLA Modules:
  0.0 55.2 jit_solution(16481767800751905366)
XLA Ops:
  0.6 0.0 copy-start.1
  0.6 1.6 %copy-done.1 = bf16[2048,512]{1,0:T(8,128)(2,1)S(1)} copy-done((bf16[2048,512]{1,0:T(8,128)(2,1)S(1)}, bf16[2048,512]{1,0:T(8,128)(2,1)}, u32[]{:S(2)}) %copy-start.1) | copy-done | bytes 2097176
  2.2 0.0 copy-start.3
  2.2 1.6 %copy-done.3 = bf16[512,2048]{1,0:T(8,128)(2,1)S(1)} copy-done((bf16[512,2048]{1,0:T(8,128)(2,1)S(1)}, bf16[512,2048]{1,0:T(8,128)(2,1)}, u32[]{:S(2)}) %copy-start.3) | copy-done | bytes 2097176
  3.8 0.0 copy-start.4
  3.8 1.2 %copy-done.4 = bf16[512,1024]{1,0:T(8,128)(2,1)S(1)} copy-done((bf16[512,1024]{1,0:T(8,128)(2,1)S(1)}, bf16[512,1024]{1,0:T(8,128)(2,1)}, u32[]{:S(2)}) %copy-start.4) | copy-done | bytes 1048600
  5.0 0.0 copy-start.5
  5.0 0.7 %copy-done.5 = f32[16,256]{1,0:T(8,128)S(1)} copy-done((f32[16,256]{1,0:T(8,128)S(1)}, f32[16,256]{1,0:T(8,128)}, u32[]{:S(2)}) %copy-start.5) | copy-done | bytes 16408
  5.8 0.0 copy-start.6
  5.8 0.7 %copy-done.6 = f32[16,256]{1,0:T(8,128)S(1)} copy-done((f32[16,256]{1,0:T(8,128)S(1)}, f32[16,256]{1,0:T(8,128)}, u32[]{:S(2)}) %copy-start.6) | copy-done | bytes 16408
  6.5 0.0 copy-start.2
  6.5 38.5 %shard_map.93 = (bf16[2,2,2,4,4,2,16,128]{7,6,5,4,3,2,1,0:T(8,128)(2,1)S(1)}, f32[16,256]{1,0:T(8,128)S(1)}, f32[16,256]{1,0:T(8,128)S(1)}) custom-call(bf16[512,2048]{1,0:T(8,128)(2,1)S(1)} %copy-done.3, bf16[512,1024]{1,0:T(8,128)(2,1)S(1)} %copy-done.4, bf16[2048,512]{1,0:T(8,128)(2,1)S(1)} %copy-done.1, f32[16,256]{1,0:T(8,128)S(1)} %copy-done.5, ...), custom_call_target="tpu_custom_call" | custom-call | tf_op jit(solution)/shard_map/pallas_call | solution.py:258
  45.0 0.0 copy-done.2
  45.0 0.0 copy-start
  45.0 3.4 %copy-done = f32[2048,1024]{1,0:T(8,128)S(1)} copy-done((f32[2048,1024]{1,0:T(8,128)S(1)}, f32[2048,1024]{1,0:T(8,128)}, u32[]{:S(2)}) %copy-start) | copy-done | bytes 8388632
  48.4 6.8 %shard_map.94 = (f32[2048,1024]{1,0:T(8,128)}, bf16[2048,1024]{1,0:T(8,128)(2,1)}, f32[16,256]{1,0:T(8,128)}, f32[16,256]{1,0:T(8,128)}) custom-call(bf16[8,512,128]{2,1,0:T(8,128)(2,1)S(1)} %bitcast.1, bf16[2048,512]{1,0:T(8,128)(2,1)S(1)} %copy-done.2, f32[2048,1024]{1,0:T(8,128)S(1)} %copy-done, f32[16,256]{1,0:T(8,128)S(1)} %get-tuple-element.8.first_in, ...), custom_call_target="tpu_custom_call" | custom-call | tf_op jit(solution)/shard_map/pallas_call | solution.py:315
Async XLA Ops:
  0.6 1.6 %copy-start.1 = (bf16[2048,512]{1,0:T(8,128)(2,1)S(1)}, bf16[2048,512]{1,0:T(8,128)(2,1)}, u32[]{:S(2)}) copy-start(bf16[2048,512]{1,0:T(8,128)(2,1)} %proj.3) | copy-start | bytes 6291460
  2.2 1.6 %copy-start.3 = (bf16[512,2048]{1,0:T(8,128)(2,1)S(1)}, bf16[512,2048]{1,0:T(8,128)(2,1)}, u32[]{:S(2)}) copy-start(bf16[512,2048]{1,0:T(8,128)(2,1)} %acts.1) | copy-start | bytes 6291460
  3.8 1.2 %copy-start.4 = (bf16[512,1024]{1,0:T(8,128)(2,1)S(1)}, bf16[512,1024]{1,0:T(8,128)(2,1)}, u32[]{:S(2)}) copy-start(bf16[512,1024]{1,0:T(8,128)(2,1)} %grads.1) | copy-start | bytes 3145732
  5.0 0.7 %copy-start.5 = (f32[16,256]{1,0:T(8,128)S(1)}, f32[16,256]{1,0:T(8,128)}, u32[]{:S(2)}) copy-start(f32[16,256]{1,0:T(8,128)} %first_moment.1) | copy-start | bytes 49156
  5.8 0.7 %copy-start.6 = (f32[16,256]{1,0:T(8,128)S(1)}, f32[16,256]{1,0:T(8,128)}, u32[]{:S(2)}) copy-start(f32[16,256]{1,0:T(8,128)} %second_moment.1) | copy-start | bytes 49156
  6.5 38.5 %copy-start.2 = (bf16[2048,512]{1,0:T(8,128)(2,1)S(1)}, bf16[2048,512]{1,0:T(8,128)(2,1)}, u32[]{:S(2)}) copy-start(bf16[2048,512]{1,0:T(8,128)(2,1)} %proj.3) | copy-start | bytes 6291460
  45.0 3.4 %copy-start = (f32[2048,1024]{1,0:T(8,128)S(1)}, f32[2048,1024]{1,0:T(8,128)}, u32[]{:S(2)}) copy-start(f32[2048,1024]{1,0:T(8,128)} %weight.1) | copy-start | bytes 25165828

commit v2 on v1

--- a/solution.py
+++ b/solution.py
@@ -18,20 +18,25 @@
 F32 = jnp.float32
 BF16 = jnp.bfloat16
 TOKEN_CHUNKS = 4
+ROW_TILE = 256
 
 
 def reduce_kernel(
     acts,
     grads,
     proj,
+    weight,
     first_moment,
     second_moment,
     gathered,
+    proj_v,
+    weight_v,
     first_new_ref,
     second_new_ref,
     acts_v,
-    proj_v,
     grads_v,
+    first_v,
+    second_v,
     mine,
     theirs,
     summed,
@@ -87,6 +92,11 @@
         )
         copy.start()
         load_grads.append(copy)
+    load_late = []
+    for n, (src, dst) in enumerate(((first_moment, first_v), (second_moment, second_v), (weight, weight_v))):
+        copy = pltpu.make_async_copy(src, dst, load_sem.at[3 + TOKEN_CHUNKS + n])
+        copy.start()
+        load_late.append(copy)
 
     barrier = pltpu.get_barrier_semaphore()
     for partner in [sibling] + [at(d) for at in (at_x, at_y, at_z) for d in (1, 2, 3)]:
@@ -188,8 +198,10 @@
         copy.wait_recv()
     coefficients = sums2[zh, zl] + got3[0] + got3[1] + got3[2]
 
-    first_new = first_decay * first_moment[...] + (1.0 - first_decay) * coefficients
-    second_new = second_decay * second_moment[...] + (1.0 - second_decay) * coefficients * coefficients
+    load_late[0].wait()
+    load_late[1].wait()
+    first_new = first_decay * first_v[...] + (1.0 - first_decay) * coefficients
+    second_new = second_decay * second_v[...] + (1.0 - second_decay) * coefficients * coefficients
     first_new_ref[...] = first_new
     second_new_ref[...] = second_new
     normalized = first_new / first_bias / (jnp.sqrt(second_new / second_bias) + epsilon)
@@ -249,25 +261,30 @@
         copy.wait_recv()
     for copy in started:
         copy.wait_send()
-
-
-def reduce_and_gather(acts, grads, proj, first_moment, second_moment):
+    load_late[2].wait()
+
+
+def reduce_and_gather(*operands):
+    proj, weight = operands[2], operands[3]
     vmem = pl.BlockSpec(memory_space=pltpu.VMEM)
-    hbm = pl.BlockSpec(memory_space=pl.ANY)
+    hbm = pl.BlockSpec(memory_space=pltpu.HBM)
     dma = pltpu.SemaphoreType.DMA
     return pl.pallas_call(
         reduce_kernel,
         out_shape=(
-            jax.ShapeDtypeStruct((2, 2, 2, 4, 4, 2, 16, 128), BF16),
-            jax.ShapeDtypeStruct((16, 256), F32),
-            jax.ShapeDtypeStruct((16, 256), F32),
+            pltpu.VMEM((2, 2, 2, 4, 4, 2, 16, 128), BF16),
+            pltpu.VMEM(proj.shape, BF16),
+            pltpu.VMEM(weight.shape, F32),
+            pltpu.VMEM((16, 256), F32),
+            pltpu.VMEM((16, 256), F32),
         ),
-        in_specs=[hbm, hbm, hbm, vmem, vmem],
-        out_specs=(vmem, vmem, vmem),
+        in_specs=[hbm] * 6,
+        out_specs=(vmem,) * 5,
         scratch_shapes=[
             pltpu.VMEM((512, 2048), BF16),
-            pltpu.VMEM((2048, 512), BF16),
             pltpu.VMEM((512, 512), BF16),
+            pltpu.VMEM((16, 256), F32),
+            pltpu.VMEM((16, 256), F32),
             pltpu.VMEM((512, 512), BF16),
             pltpu.VMEM((512, 512), BF16),
             pltpu.VMEM((512, 512), F32),
@@ -277,7 +294,7 @@
             pltpu.VMEM((2, 3, 2, 32, 128), BF16),
             pltpu.VMEM((2, 2, 16, 256), F32),
             pltpu.VMEM((3, 16, 256), F32),
-            dma((3 + TOKEN_CHUNKS,)),
+            dma((6 + TOKEN_CHUNKS,)),
             dma((TOKEN_CHUNKS,)),
             dma((TOKEN_CHUNKS,)),
             dma((3, 2, 3)),
@@ -290,57 +307,84 @@
         compiler_params=pltpu.CompilerParams(
             collective_id=0, has_side_effects=True, vmem_limit_bytes=24 * 1024 * 1024
         ),
-    )(acts, grads, proj, first_moment, second_moment)
-
-
-def expand_kernel(gathered, proj, weight, first_in, second_in, new_weight, update, first_out, second_out):
-    @pl.when(pl.program_id(0) == 0)
-    def _():
-        first_out[...] = first_in[...]
-        second_out[...] = second_in[...]
-
-    rows = proj[...]
-    for n in range(4):
-        columns = slice(n * 256, (n + 1) * 256)
-        block = jnp.concatenate([gathered[2 * n], gathered[2 * n + 1]], axis=1)
-        expanded = jnp.dot(rows, block, preferred_element_type=F32)
-        new_weight[:, columns] = weight[:, columns] - step_rate * expanded
-        update[:, columns] = expanded.astype(BF16)
+    )(*(pltpu.with_memory_space_constraint(a, pltpu.HBM) for a in operands))
+
+
+def expand_kernel(
+    gathered,
+    proj,
+    weight,
+    first_in,
+    second_in,
+    new_weight,
+    update,
+    first_out,
+    second_out,
+    new_v,
+    update_v,
+    sems,
+    state_sems,
+):
+    states = [
+        pltpu.make_async_copy(first_in, first_out, state_sems.at[0]),
+        pltpu.make_async_copy(second_in, second_out, state_sems.at[1]),
+    ]
+    for copy in states:
+        copy.start()
+
+    def stores(i):
+        rows = pl.ds(i * ROW_TILE, ROW_TILE)
+        return (
+            pltpu.make_async_copy(new_v.at[rows], new_weight.at[rows], sems.at[0, i]),
+            pltpu.make_async_copy(update_v.at[rows], update.at[rows], sems.at[1, i]),
+        )
+
+    tiles = weight.shape[0] // ROW_TILE
+    for i in range(tiles):
+        rows = pl.ds(i * ROW_TILE, ROW_TILE)
+        left = proj[rows, :]
+        for n in range(4):
+            columns = slice(n * 256, (n + 1) * 256)
+            block = jnp.concatenate([gathered[2 * n], gathered[2 * n + 1]], axis=1)
+            expanded = jnp.dot(left, block, preferred_element_type=F32)
+            new_v[rows, columns] = weight[rows, columns] - step_rate * expanded
+            update_v[rows, columns] = expanded.astype(BF16)
+        for copy in stores(i):
+            copy.start()
+    for i in range(tiles):
+        for copy in stores(i):
+            copy.wait()
+    for copy in states:
+        copy.wait()
 
 
 def expand(gathered, proj, weight, first_new, second_new):
     depth, rank = proj.shape
-    tile = 256
-    whole = lambda *shape: pl.BlockSpec(shape, lambda i: (0,) * len(shape))
+    vmem = pl.BlockSpec(memory_space=pltpu.VMEM)
+    hbm = pl.BlockSpec(memory_space=pltpu.HBM)
     return pl.pallas_call(
         expand_kernel,
-        grid=(depth // tile,),
         out_shape=(
             jax.ShapeDtypeStruct((depth, 1024), F32),
             jax.ShapeDtypeStruct((depth, 1024), BF16),
             jax.ShapeDtypeStruct((16, 256), F32),
             jax.ShapeDtypeStruct((16, 256), F32),
         ),
-        in_specs=[
-            whole(8, rank, 128),
-            pl.BlockSpec((tile, rank), lambda i: (i, 0)),
-            pl.BlockSpec((tile, 1024), lambda i: (i, 0)),
-            whole(16, 256),
-            whole(16, 256),
+        in_specs=[vmem] * 5,
+        out_specs=(hbm,) * 4,
+        scratch_shapes=[
+            pltpu.VMEM((depth, 1024), F32),
+            pltpu.VMEM((depth, 1024), BF16),
+            pltpu.SemaphoreType.DMA((2, depth // ROW_TILE)),
+            pltpu.SemaphoreType.DMA((2,)),
         ],
-        out_specs=(
-            pl.BlockSpec((tile, 1024), lambda i: (i, 0)),
-            pl.BlockSpec((tile, 1024), lambda i: (i, 0)),
-            whole(16, 256),
-            whole(16, 256),
-        ),
-        compiler_params=pltpu.CompilerParams(vmem_limit_bytes=16 * 1024 * 1024),
+        compiler_params=pltpu.CompilerParams(vmem_limit_bytes=20 * 1024 * 1024),
     )(gathered, proj, weight, first_new, second_new)
 
 
 def local(activations, out_grads, projector, weight, first_moment, second_moment):
-    gathered, first_new, second_new = reduce_and_gather(
-        activations, out_grads, projector, first_moment, second_moment
+    gathered, projector, weight, first_new, second_new = reduce_and_gather(
+        activations, out_grads, projector, weight, first_moment, second_moment
     )
     gathered = gathered.reshape(8, 512, 128)
     return tuple(expand(gathered, projector, weight, first_new, second_new))

time: 55.6 us -> 44.2 us (0.79)
  local copies, waits for them, and re-layouts: 9.21 us -> 0 us
  Pallas kernels: 45.3 us -> 43.5 us
    unnamed x14 -> x0, local copies, waits for them, and re-layouts: 9.21 us -> none
    pallas_call x2, Pallas kernels: 45.3 us -> 43.5 us  [the longest x1 38.3 us: reduce_and_gather(): pl.pallas_call(reduce_kernel, out_shape=(pltpu.VMEM((2, 2, 2, 4, 4, 2, 16...]
where the time goes in v2:
time: 44.2 us; the launch traced here: 44.1 us
  Pallas kernels  43.5 us (98%)
  between operations  0.64 us (1%)
    pallas_call x1, Pallas kernels, reduce_and_gather(): pl.pallas_call(reduce_kernel, out_shape=(pltpu.VMEM((2, 2, 2, 4, 4, 2, 16...  38.3 us
    pallas_call x1, Pallas kernels, expand(): pl.pallas_call(expand_kernel, out_shape=(jax.ShapeDtypeStruct((depth, 102...  5.16 us

profile of v2, /device:TPU:1, one launch (start us, length us, event | category | flops | bytes accessed | tf_op | source)
XLA Modules:
  0.0 44.1 jit_solution(7757315421571332958)
XLA Ops:
  0.6 38.3 %shard_map.93 = (bf16[2,2,2,4,4,2,16,128]{7,6,5,4,3,2,1,0:T(8,128)(2,1)S(1)}, bf16[2048,512]{1,0:T(8,128)(2,1)S(1)}, f32[2048,1024]{1,0:T(8,128)S(1)}, f32[16,256]{1,0:T(8,128)S(1)}, f32[16,256]{1,0:T(8,128)S(1)}) custom-call(bf16[512,2048]{1,0:T(8,128)(2,1)} %acts.1, bf16[512,1024]{1,0:T(8,128)(2,1)} %grads.1, bf16[2048,512]{1,0:T(8,128)(2,1)} %proj.1, ...), custom_call_target="tpu_custom_call" | custom-call | tf_op jit(solution)/shard_map/pallas_call | solution.py:272
  39.0 5.2 %shard_map.94 = (f32[2048,1024]{1,0:T(8,128)}, bf16[2048,1024]{1,0:T(8,128)(2,1)}, f32[16,256]{1,0:T(8,128)}, f32[16,256]{1,0:T(8,128)}) custom-call(bf16[8,512,128]{2,1,0:T(8,128)(2,1)S(1)} %bitcast.1, bf16[2048,512]{1,0:T(8,128)(2,1)S(1)} %get-tuple-element.10.proj, f32[2048,1024]{1,0:T(8,128)S(1)} %get-tuple-element.11.weight, ...), custom_call_target="tpu_custom_call" | custom-call | tf_op jit(solution)/shard_map/pallas_call | solution.py:365

commit v3 on v2

v3 whole, which is shorter than its diff:
```python
import functools

import jax
import jax.numpy as jnp
from jax import lax
from jax.experimental import pallas as pl
from jax.experimental.pallas import tpu as pltpu
from jax.sharding import PartitionSpec as P

first_decay = 0.9
second_decay = 0.999
first_bias = 1.0 - 0.9**2
second_bias = 1.0 - 0.999**2
epsilon = 1e-08
step_rate = 0.00025

MESH = pl.DeviceIdType.MESH
F32 = jnp.float32
BF16 = jnp.bfloat16
TOKEN_CHUNKS = 4
ROW_TILE = 256


def place(half, v):
    return ((v + v // 2) % 2, v // 2) if half == 0 else (v // 2, v % 2)


MASKS = (7, 6, 5, 3, 4, 2, 1)


def bits(m):
    return m // 4, m // 2 % 2, m % 2


def reduce_kernel(
    acts,
    grads,
    proj,
    weight,
    first_moment,
    second_moment,
    gathered,
    proj_v,
    weight_v,
    first_new_ref,
    second_new_ref,
    acts_v,
    grads_v,
    first_v,
    second_v,
    mine,
    theirs,
    both,
    summed,
    parts,
    got1,
    sums,
    got2,
    load_sem,
    pair_send,
    pair_recv,
    rs_send,
    rs_recv,
    ag_send,
    ag_recv,
    fw_send,
    fw_recv,
):
    dp = lax.axis_index("dp")
    mp = lax.axis_index("mp")
    zh, c = mp // 2, mp % 2
    chip = (dp // 8, (dp // 2) % 4, zh * 2 + dp % 2)
    sibling = (dp, zh * 2 + 1 - c)

    def partner(wrap, m):
        x, y, z = ((3 - v if wrap else v + 1 - 2 * (v % 2)) if bit else v for v, bit in zip(chip, bits(m)))
        return (x * 8 + y * 2 + z % 2, (z // 2) * 2 + c)

    def flip(at, m):
        return tuple(1 - v if bit else v for v, bit in zip(at, bits(m)))

    sets, members = [], []
    for half in range(2):
        places = [place(half, v) for v in chip]
        sets.append(tuple(p[0] for p in places))
        members.append(tuple(p[1] for p in places))

    tokens = acts.shape[0]
    chunk = tokens // TOKEN_CHUNKS
    load_proj = pltpu.make_async_copy(proj, proj_v, load_sem.at[0])
    load_proj.start()
    load_acts = []
    for t in range(TOKEN_CHUNKS):
        rows = pl.ds(t * chunk, chunk)
        copy = pltpu.make_async_copy(acts.at[rows], acts_v.at[rows], load_sem.at[1 + t])
        copy.start()
        load_acts.append(copy)
    load_grads = []
    for h in range(2):
        columns = pl.ds(pl.multiple_of(h * 512 + c * 256, 256), 256)
        copy = pltpu.make_async_copy(
            grads.at[:, columns], grads_v.at[:, pl.ds(h * 256, 256)], load_sem.at[1 + TOKEN_CHUNKS + h]
        )
        copy.start()
        load_grads.append(copy)
    load_late = [
        pltpu.make_async_copy(src, dst, load_sem.at[3 + TOKEN_CHUNKS + n])
        for n, (src, dst) in enumerate(((first_moment, first_v), (second_moment, second_v), (weight, weight_v)))
    ]
    load_late[0].start()
    load_late[1].start()

    barrier = pltpu.get_barrier_semaphore()
    for device in [sibling] + [partner(wrap, m) for wrap in (False, True) for m in MASKS]:
        pl.semaphore_signal(barrier, inc=1, device_id=device, device_id_type=MESH)

    started = []

    def send(src, dst, send_sem, recv_sem, device):
        copy = pltpu.make_async_remote_copy(
            src_ref=src, dst_ref=dst, send_sem=send_sem, recv_sem=recv_sem, device_id=device, device_id_type=MESH
        )
        copy.start()
        started.append(copy)
        return copy

    load_proj.wait()
    pair = []
    for t in range(TOKEN_CHUNKS):
        rows = pl.ds(t * chunk, chunk)
        load_acts[t].wait()
        projected = jnp.dot(acts_v[rows, :], proj_v[...], preferred_element_type=F32)
        mine[rows, :] = projected.astype(BF16)
        summed[rows, :] = projected
        if t == 0:
            pl.semaphore_wait(barrier, 15)
        pair.append(send(mine.at[rows], theirs.at[rows], pair_send.at[t], pair_recv.at[t], sibling))
    for copy in load_grads:
        copy.wait()
    load_late[2].start()
    for t in range(TOKEN_CHUNKS):
        rows = pl.ds(t * chunk, chunk)
        pair[t].wait_recv()
        both[rows, :] = (summed[rows, :] + theirs[rows, :].astype(F32)).astype(BF16)

    for x in range(4):
        block = lax.dot_general(
            both[:, x * 128 : (x + 1) * 128],
            grads_v[...],
            (((0,), (0,)), ((), ())),
            preferred_element_type=F32,
        ).astype(BF16)
        for y in range(4):
            for z in range(4):
                row = y * 32 + z % 2 * 16
                for half in range(2):
                    column = z // 2 * 256 + half * 128
                    at = [place(half, v) for v in (x, y, z)]
                    index = tuple(p[0] for p in at) + tuple(p[1] for p in at)
                    parts[(half, *index)] = block[row : row + 16, column : column + 128]

    stage1 = ([], [])
    for n, m in enumerate(MASKS):
        for half in range(2):
            to = flip(sets[half], m)
            stage1[half].append(
                send(
                    parts.at[(half, *to)],
                    got1.at[half, n],
                    rs_send.at[0, half, n],
                    rs_recv.at[0, half, n],
                    partner(half == 1, m),
                )
            )
    stage2 = ([], [])
    for half in range(2):
        for copy in stage1[half]:
            copy.wait_recv()
        total = parts[(half, *sets[half])].astype(F32)
        for n in range(7):
            total += got1[half, n].astype(F32)
        sums[half] = total.astype(BF16)
        for n, m in enumerate(MASKS):
            to = flip(members[half], m)
            stage2[half].append(
                send(
                    sums.at[(half, *to)],
                    got2.at[half, n],
                    rs_send.at[1, half, n],
                    rs_recv.at[1, half, n],
                    partner(half == 0, m),
                )
            )
    load_late[0].wait()
    load_late[1].wait()
    gather1 = ([], [])
    for half in range(2):
        for copy in stage2[half]:
            copy.wait_recv()
        coefficients = sums[(half, *members[half])].astype(F32)
        for n in range(7):
            coefficients += got2[half, n].astype(F32)

        columns = slice(half * 128, (half + 1) * 128)
        first_new = first_decay * first_v[:, columns] + (1.0 - first_decay) * coefficients
        second_new = second_decay * second_v[:, columns] + (1.0 - second_decay) * coefficients * coefficients
        first_new_ref[:, columns] = first_new
        second_new_ref[:, columns] = second_new
        normalized = first_new / first_bias / (jnp.sqrt(second_new / second_bias) + epsilon)
        own = (c, half, *sets[half], *members[half])
        gathered[own] = normalized.astype(BF16)

        for n, m in enumerate(MASKS):
            block = gathered.at[own]
            gather1[half].append(
                send(block, block, ag_send.at[0, half, n], ag_recv.at[0, half, n], partner(half == 0, m))
            )
    gather2 = ([], [])
    forwards = []

    def forward(half, at, n):
        block = gathered.at[(c, half, *at)]
        forwards.append(send(block, block, fw_send.at[half, n], fw_recv.at[half, n], sibling))

    for half in range(2):
        for copy in gather1[half]:
            copy.wait_recv()
        block = gathered.at[(c, half, *sets[half])]
        for n, m in enumerate(MASKS):
            gather2[half].append(
                send(block, block, ag_send.at[1, half, n], ag_recv.at[1, half, n], partner(half == 1, m))
            )
        forward(half, sets[half], 7)
    for n in reversed(range(7)):
        for half in range(2):
            gather2[half][n].wait_recv()
            forward(half, flip(sets[half], MASKS[n]), n)
    for copy in forwards:
        copy.wait_recv()
    for copy in started:
        copy.wait_send()
    load_late[2].wait()


def reduce_and_gather(*operands):
    proj, weight = operands[2], operands[3]
    vmem = pl.BlockSpec(memory_space=pltpu.VMEM)
    hbm = pl.BlockSpec(memory_space=pltpu.HBM)
    dma = pltpu.SemaphoreType.DMA
    return pl.pallas_call(
        reduce_kernel,
        out_shape=(
            pltpu.VMEM((2, 2, 2, 2, 2, 2, 2, 2, 16, 128), BF16),
            pltpu.VMEM(proj.shape, BF16),
            pltpu.VMEM(weight.shape, F32),
            pltpu.VMEM((16, 256), F32),
            pltpu.VMEM((16, 256), F32),
        ),
        in_specs=[hbm] * 6,
        out_specs=(vmem,) * 5,
        scratch_shapes=[
            pltpu.VMEM((512, 2048), BF16),
            pltpu.VMEM((512, 512), BF16),
            pltpu.VMEM((16, 256), F32),
            pltpu.VMEM((16, 256), F32),
            pltpu.VMEM((512, 512), BF16),
            pltpu.VMEM((512, 512), BF16),
            pltpu.VMEM((512, 512), BF16),
            pltpu.VMEM((512, 512), F32),
            pltpu.VMEM((2, 2, 2, 2, 2, 2, 2, 16, 128), BF16),
            pltpu.VMEM((2, 7, 2, 2, 2, 16, 128), BF16),
            pltpu.VMEM((2, 2, 2, 2, 16, 128), BF16),
            pltpu.VMEM((2, 7, 16, 128), BF16),
            dma((6 + TOKEN_CHUNKS,)),
            dma((TOKEN_CHUNKS,)),
            dma((TOKEN_CHUNKS,)),
            dma((2, 2, 7)),
            dma((2, 2, 7)),
            dma((2, 2, 7)),
            dma((2, 2, 7)),
            dma((2, 8)),
            dma((2, 8)),
        ],
        compiler_params=pltpu.CompilerParams(
            collective_id=0, has_side_effects=True, vmem_limit_bytes=24 * 1024 * 1024
        ),
    )(*(pltpu.with_memory_space_constraint(a, pltpu.HBM) for a in operands))


def expand_kernel(
    gathered,
    proj,
    weight,
    first_in,
    second_in,
    new_weight,
    update,
    first_out,
    second_out,
    ordered,
    new_v,
    update_v,
    sems,
    state_sems,
):
    states = [
        pltpu.make_async_copy(first_in, first_out, state_sems.at[0]),
        pltpu.make_async_copy(second_in, second_out, state_sems.at[1]),
    ]
    for copy in states:
        copy.start()

    def stores(i):
        rows = pl.ds(i * ROW_TILE, ROW_TILE)
        return (
            pltpu.make_async_copy(new_v.at[rows], new_weight.at[rows], sems.at[0, i]),
            pltpu.make_async_copy(update_v.at[rows], update.at[rows], sems.at[1, i]),
        )

    for zh in range(2):
        for c in range(2):
            for half in range(2):
                column = zh * 512 + c * 256 + half * 128
                for x in range(4):
                    for y in range(4):
                        for zl in range(2):
                            at = [place(half, v) for v in (x, y, zh * 2 + zl)]
                            index = tuple(p[0] for p in at) + tuple(p[1] for p in at)
                            row = x * 128 + y * 32 + zl * 16
                            ordered[row : row + 16, column : column + 128] = gathered[(c, half, *index)]

    tiles = weight.shape[0] // ROW_TILE
    for i in range(tiles):
        rows = pl.ds(i * ROW_TILE, ROW_TILE)
        left = proj[rows, :]
        for n in range(4):
            columns = slice(n * 256, (n + 1) * 256)
            expanded = jnp.dot(left, ordered[:, columns], preferred_element_type=F32)
            new_v[rows, columns] = weight[rows, columns] - step_rate * expanded
            update_v[rows, columns] = expanded.astype(BF16)
        for copy in stores(i):
            copy.start()
    for i in range(tiles):
        for copy in stores(i):
            copy.wait()
    for copy in states:
        copy.wait()


def expand(gathered, proj, weight, first_new, second_new):
    depth, rank = proj.shape
    vmem = pl.BlockSpec(memory_space=pltpu.VMEM)
    hbm = pl.BlockSpec(memory_space=pltpu.HBM)
    return pl.pallas_call(
        expand_kernel,
        out_shape=(
            jax.ShapeDtypeStruct((depth, 1024), F32),
            jax.ShapeDtypeStruct((depth, 1024), BF16),
            jax.ShapeDtypeStruct((16, 256), F32),
            jax.ShapeDtypeStruct((16, 256), F32),
        ),
        in_specs=[vmem] * 5,
        out_specs=(hbm,) * 4,
        scratch_shapes=[
            pltpu.VMEM((rank, 1024), BF16),
            pltpu.VMEM((depth, 1024), F32),
            pltpu.VMEM((depth, 1024), BF16),
            pltpu.SemaphoreType.DMA((2, depth // ROW_TILE)),
            pltpu.SemaphoreType.DMA((2,)),
        ],
        compiler_params=pltpu.CompilerParams(vmem_limit_bytes=20 * 1024 * 1024),
    )(gathered, proj, weight, first_new, second_new)


def local(activations, out_grads, projector, weight, first_moment, second_moment):
    gathered, projector, weight, first_new, second_new = reduce_and_gather(
        activations, out_grads, projector, weight, first_moment, second_moment
    )
    return tuple(expand(gathered, projector, weight, first_new, second_new))


def solution(mesh):
    in_specs = (
        P("dp", "mp"),
        P("dp", None),
        P("mp", None),
        P("mp", None),
        P("dp", "mp"),
        P("dp", "mp"),
    )
    out_specs = (P("mp", None), P("mp", None), P("dp", "mp"), P("dp", "mp"))
    return jax.shard_map(local, mesh=mesh, in_specs=in_specs, out_specs=out_specs, check_vma=False)
```

time: 44.2 us -> 40.9 us (0.925)
  Pallas kernels: 43.5 us -> 40.1 us
    pallas_call x1, Pallas kernels: 38.3 us -> 34.9 us  [reduce_and_gather(): pl.pallas_call(reduce_kernel, out_shape=(pltpu.VMEM((2, 2, 2, 2, 2, 2, 2,...]
where the time goes in v3:
time: 40.9 us; the launch traced here: 40.8 us
  Pallas kernels  40.1 us (98%)
  between operations  0.64 us (2%)
    pallas_call x1, Pallas kernels, reduce_and_gather(): pl.pallas_call(reduce_kernel, out_shape=(pltpu.VMEM((2, 2, 2, 2, 2, 2, 2,...  34.9 us
    pallas_call x1, Pallas kernels, expand(): pl.pallas_call(expand_kernel, out_shape=(jax.ShapeDtypeStruct((depth, 102...  5.23 us

profile of v3, /device:TPU:1, one launch (start us, length us, event | category | flops | bytes accessed | tf_op | source)
XLA Modules:
  0.0 40.8 jit_solution(16530115358294650356)
XLA Ops:
  0.6 34.9 %shard_map.93 = (bf16[2,2,2,2,2,2,2,2,16,128]{9,8,7,6,5,4,3,2,1,0:T(8,128)(2,1)S(1)}, bf16[2048,512]{1,0:T(8,128)(2,1)S(1)}, f32[2048,1024]{1,0:T(8,128)S(1)}, f32[16,256]{1,0:T(8,128)S(1)}, f32[16,256]{1,0:T(8,128)S(1)}) custom-call(bf16[512,2048]{1,0:T(8,128)(2,1)} %acts.1, bf16[512,1024]{1,0:T(8,128)(2,1)} %grads.1, bf16[2048,512]{1,0:T(8,128)(2,1)} %proj.1, ...), custom_call_target="tpu_custom_call" | custom-call | tf_op jit(solution)/shard_map/pallas_call | solution.py:250
  35.6 5.2 %shard_map.94 = (f32[2048,1024]{1,0:T(8,128)}, bf16[2048,1024]{1,0:T(8,128)(2,1)}, f32[16,256]{1,0:T(8,128)}, f32[16,256]{1,0:T(8,128)}) custom-call(bf16[2,2,2,2,2,2,2,2,16,128]{9,8,7,6,5,4,3,2,1,0:T(8,128)(2,1)S(1)} %get-tuple-element.9.gathered, bf16[2048,512]{1,0:T(8,128)(2,1)S(1)} %get-tuple-element.10.proj, f32[2048,1024]{1,0:T(8,128)S(1)} %get-tuple-element.11.weight, ...), custom_call_target="tpu_custom_call" | custom-call | tf_op jit(solution)/shard_map/pallas_call | solution.py:354

commit v4 on v3

--- a/solution.py
+++ b/solution.py
@@ -46,8 +46,6 @@
     second_new_ref,
     acts_v,
     grads_v,
-    first_v,
-    second_v,
     mine,
     theirs,
     both,
@@ -55,14 +53,13 @@
     parts,
     got1,
     sums,
-    got2,
+    moments,
+    states,
     load_sem,
     pair_send,
     pair_recv,
-    rs_send,
-    rs_recv,
-    ag_send,
-    ag_recv,
+    send_sem,
+    recv_sem,
     fw_send,
     fw_recv,
 ):
@@ -96,19 +93,28 @@
         copy.start()
         load_acts.append(copy)
     load_grads = []
-    for h in range(2):
-        columns = pl.ds(pl.multiple_of(h * 512 + c * 256, 256), 256)
-        copy = pltpu.make_async_copy(
-            grads.at[:, columns], grads_v.at[:, pl.ds(h * 256, 256)], load_sem.at[1 + TOKEN_CHUNKS + h]
-        )
-        copy.start()
-        load_grads.append(copy)
-    load_late = [
-        pltpu.make_async_copy(src, dst, load_sem.at[3 + TOKEN_CHUNKS + n])
-        for n, (src, dst) in enumerate(((first_moment, first_v), (second_moment, second_v), (weight, weight_v)))
-    ]
-    load_late[0].start()
-    load_late[1].start()
+    for half in range(2):
+        for h in range(2):
+            columns = pl.ds(pl.multiple_of(h * 512 + c * 256 + half * 128, 128), 128)
+            copy = pltpu.make_async_copy(
+                grads.at[:, columns],
+                grads_v.at[half, :, pl.ds(h * 128, 128)],
+                load_sem.at[1 + TOKEN_CHUNKS + 2 * half + h],
+            )
+            copy.start()
+            load_grads.append(copy)
+    load_moments = []
+    for half in range(2):
+        columns = pl.ds(half * 128, 128)
+        for n, moment in enumerate((first_moment, second_moment)):
+            copy = pltpu.make_async_copy(
+                moment.at[:, columns],
+                moments.at[(half, *members[half], n)],
+                load_sem.at[5 + TOKEN_CHUNKS + 2 * half + n],
+            )
+            copy.start()
+            load_moments.append(copy)
+    load_weight = pltpu.make_async_copy(weight, weight_v, load_sem.at[9 + TOKEN_CHUNKS])
 
     barrier = pltpu.get_barrier_semaphore()
     for device in [sibling] + [partner(wrap, m) for wrap in (False, True) for m in MASKS]:
@@ -116,13 +122,22 @@
 
     started = []
 
-    def send(src, dst, send_sem, recv_sem, device):
+    def send(src, dst, sent, arrived, device):
         copy = pltpu.make_async_remote_copy(
-            src_ref=src, dst_ref=dst, send_sem=send_sem, recv_sem=recv_sem, device_id=device, device_id_type=MESH
+            src_ref=src, dst_ref=dst, send_sem=sent, recv_sem=arrived, device_id=device, device_id_type=MESH
         )
         copy.start()
         started.append(copy)
         return copy
+
+    def spread(stage, half, flips, source, target=None):
+        copies = []
+        for n, m in enumerate(MASKS):
+            src = source(m)
+            dst = src if target is None else target(n)
+            device = partner((half == 1) == (flips == 1), m)
+            copies.append(send(src, dst, send_sem.at[stage, half, n], recv_sem.at[stage, half, n], device))
+        return copies
 
     load_proj.wait()
     pair = []
@@ -135,111 +150,91 @@
         if t == 0:
             pl.semaphore_wait(barrier, 15)
         pair.append(send(mine.at[rows], theirs.at[rows], pair_send.at[t], pair_recv.at[t], sibling))
+    for copy in load_moments:
+        copy.wait()
+    gather0 = [
+        spread(0, half, 2, lambda m, half=half: moments.at[(half, *members[half])]) for half in range(2)
+    ]
     for copy in load_grads:
         copy.wait()
-    load_late[2].start()
+    load_weight.start()
     for t in range(TOKEN_CHUNKS):
         rows = pl.ds(t * chunk, chunk)
         pair[t].wait_recv()
-        both[rows, :] = (summed[rows, :] + theirs[rows, :].astype(F32)).astype(BF16)
-
-    for x in range(4):
-        block = lax.dot_general(
-            both[:, x * 128 : (x + 1) * 128],
-            grads_v[...],
-            (((0,), (0,)), ((), ())),
-            preferred_element_type=F32,
-        ).astype(BF16)
-        for y in range(4):
-            for z in range(4):
-                row = y * 32 + z % 2 * 16
-                for half in range(2):
-                    column = z // 2 * 256 + half * 128
+        both[:, t * chunk : (t + 1) * chunk] = (summed[rows, :] + theirs[rows, :].astype(F32)).T.astype(BF16)
+
+    stage1 = []
+    for half in range(2):
+        block = jnp.dot(both[...], grads_v[half], preferred_element_type=F32).astype(BF16)
+        for x in range(4):
+            for y in range(4):
+                for z in range(4):
+                    row, column = x * 128 + y * 32 + z % 2 * 16, z // 2 * 128
                     at = [place(half, v) for v in (x, y, z)]
                     index = tuple(p[0] for p in at) + tuple(p[1] for p in at)
                     parts[(half, *index)] = block[row : row + 16, column : column + 128]
-
-    stage1 = ([], [])
-    for n, m in enumerate(MASKS):
-        for half in range(2):
-            to = flip(sets[half], m)
-            stage1[half].append(
-                send(
-                    parts.at[(half, *to)],
-                    got1.at[half, n],
-                    rs_send.at[0, half, n],
-                    rs_recv.at[0, half, n],
-                    partner(half == 1, m),
-                )
+        stage1.append(
+            spread(
+                1,
+                half,
+                1,
+                lambda m: parts.at[(half, *flip(sets[half], m))],
+                lambda n: got1.at[half, n],
             )
-    stage2 = ([], [])
+        )
+
+    stage2 = []
     for half in range(2):
         for copy in stage1[half]:
             copy.wait_recv()
         total = parts[(half, *sets[half])].astype(F32)
         for n in range(7):
             total += got1[half, n].astype(F32)
-        sums[half] = total.astype(BF16)
-        for n, m in enumerate(MASKS):
-            to = flip(members[half], m)
-            stage2[half].append(
-                send(
-                    sums.at[(half, *to)],
-                    got2.at[half, n],
-                    rs_send.at[1, half, n],
-                    rs_recv.at[1, half, n],
-                    partner(half == 0, m),
-                )
-            )
-    load_late[0].wait()
-    load_late[1].wait()
-    gather1 = ([], [])
-    for half in range(2):
+        own = (half, *members[half])
+        sums[own] = total.astype(BF16)
+        stage2.append(spread(2, half, 2, lambda m: sums.at[own]))
+
+    gather2 = []
+    for half in range(2):
+        for copy in gather0[half]:
+            copy.wait_recv()
         for copy in stage2[half]:
             copy.wait_recv()
-        coefficients = sums[(half, *members[half])].astype(F32)
-        for n in range(7):
-            coefficients += got2[half, n].astype(F32)
-
+        for i in range(2):
+            for j in range(2):
+                for k in range(2):
+                    coefficients = sums[half, 0, 0, 0, i, j, k].astype(F32)
+                    for n in range(1, 8):
+                        coefficients += sums[(half, *bits(n), i, j, k)].astype(F32)
+                    first_new = first_decay * moments[half, i, j, k, 0] + (1.0 - first_decay) * coefficients
+                    second_new = (
+                        second_decay * moments[half, i, j, k, 1]
+                        + (1.0 - second_decay) * coefficients * coefficients
+                    )
+                    normalized = first_new / first_bias / (jnp.sqrt(second_new / second_bias) + epsilon)
+                    gathered[(c, half, *sets[half], i, j, k)] = normalized.astype(BF16)
+                    states[half, i, j, k, 0] = first_new
+                    states[half, i, j, k, 1] = second_new
+        gather2.append(spread(3, half, 1, lambda m: gathered.at[(c, half, *sets[half])]))
+    for half in range(2):
         columns = slice(half * 128, (half + 1) * 128)
-        first_new = first_decay * first_v[:, columns] + (1.0 - first_decay) * coefficients
-        second_new = second_decay * second_v[:, columns] + (1.0 - second_decay) * coefficients * coefficients
-        first_new_ref[:, columns] = first_new
-        second_new_ref[:, columns] = second_new
-        normalized = first_new / first_bias / (jnp.sqrt(second_new / second_bias) + epsilon)
-        own = (c, half, *sets[half], *members[half])
-        gathered[own] = normalized.astype(BF16)
-
-        for n, m in enumerate(MASKS):
-            block = gathered.at[own]
-            gather1[half].append(
-                send(block, block, ag_send.at[0, half, n], ag_recv.at[0, half, n], partner(half == 0, m))
-            )
-    gather2 = ([], [])
+        first_new_ref[:, columns] = states[(half, *members[half], 0)]
+        second_new_ref[:, columns] = states[(half, *members[half], 1)]
+
     forwards = []
-
-    def forward(half, at, n):
-        block = gathered.at[(c, half, *at)]
-        forwards.append(send(block, block, fw_send.at[half, n], fw_recv.at[half, n], sibling))
-
-    for half in range(2):
-        for copy in gather1[half]:
-            copy.wait_recv()
-        block = gathered.at[(c, half, *sets[half])]
-        for n, m in enumerate(MASKS):
-            gather2[half].append(
-                send(block, block, ag_send.at[1, half, n], ag_recv.at[1, half, n], partner(half == 1, m))
-            )
-        forward(half, sets[half], 7)
-    for n in reversed(range(7)):
+    for far in range(2):
         for half in range(2):
-            gather2[half][n].wait_recv()
-            forward(half, flip(sets[half], MASKS[n]), n)
+            for n, m in enumerate(MASKS):
+                if m // 4 == far:
+                    gather2[half][n].wait_recv()
+            x = sets[half][0]
+            block = gathered.at[c, half, 1 - x if far else x]
+            forwards.append(send(block, block, fw_send.at[half, far], fw_recv.at[half, far], sibling))
     for copy in forwards:
         copy.wait_recv()
     for copy in started:
         copy.wait_send()
-    load_late[2].wait()
+    load_weight.wait()
 
 
 def reduce_and_gather(*operands):
@@ -260,26 +255,23 @@
         out_specs=(vmem,) * 5,
         scratch_shapes=[
             pltpu.VMEM((512, 2048), BF16),
-            pltpu.VMEM((512, 512), BF16),
-            pltpu.VMEM((16, 256), F32),
-            pltpu.VMEM((16, 256), F32),
+            pltpu.VMEM((2, 512, 256), BF16),
             pltpu.VMEM((512, 512), BF16),
             pltpu.VMEM((512, 512), BF16),
             pltpu.VMEM((512, 512), BF16),
             pltpu.VMEM((512, 512), F32),
             pltpu.VMEM((2, 2, 2, 2, 2, 2, 2, 16, 128), BF16),
             pltpu.VMEM((2, 7, 2, 2, 2, 16, 128), BF16),
-            pltpu.VMEM((2, 2, 2, 2, 16, 128), BF16),
-            pltpu.VMEM((2, 7, 16, 128), BF16),
-            dma((6 + TOKEN_CHUNKS,)),
+            pltpu.VMEM((2, 2, 2, 2, 2, 2, 2, 16, 128), BF16),
+            pltpu.VMEM((2, 2, 2, 2, 2, 16, 128), F32),
+            pltpu.VMEM((2, 2, 2, 2, 2, 16, 128), F32),
+            dma((10 + TOKEN_CHUNKS,)),
             dma((TOKEN_CHUNKS,)),
             dma((TOKEN_CHUNKS,)),
-            dma((2, 2, 7)),
-            dma((2, 2, 7)),
-            dma((2, 2, 7)),
-            dma((2, 2, 7)),
-            dma((2, 8)),
-            dma((2, 8)),
+            dma((4, 2, 7)),
+            dma((4, 2, 7)),
+            dma((2, 2)),
+            dma((2, 2)),
         ],
         compiler_params=pltpu.CompilerParams(
             collective_id=0, has_side_effects=True, vmem_limit_bytes=24 * 1024 * 1024

time: 40.9 us -> 37.5 us (0.917)
  Pallas kernels: 40.1 us -> 36.7 us
    pallas_call x1, Pallas kernels: 34.9 us -> 31.5 us  [reduce_and_gather(): pl.pallas_call(reduce_kernel, out_shape=(pltpu.VMEM((2, 2, 2, 2, 2, 2, 2,...]
where the time goes in v4:
time: 37.5 us; the launch traced here: 37.4 us
  Pallas kernels  36.7 us (98%)
  between operations  0.64 us (2%)
    pallas_call x1, Pallas kernels, reduce_and_gather(): pl.pallas_call(reduce_kernel, out_shape=(pltpu.VMEM((2, 2, 2, 2, 2, 2, 2,...  31.5 us
    pallas_call x1, Pallas kernels, expand(): pl.pallas_call(expand_kernel, out_shape=(jax.ShapeDtypeStruct((depth, 102...  5.23 us

profile of v4, /device:TPU:1, one launch (start us, length us, event | category | flops | bytes accessed | tf_op | source)
XLA Modules:
  0.0 37.4 jit_solution(12376735367590072535)
XLA Ops:
  0.6 31.5 %shard_map.93 = (bf16[2,2,2,2,2,2,2,2,16,128]{9,8,7,6,5,4,3,2,1,0:T(8,128)(2,1)S(1)}, bf16[2048,512]{1,0:T(8,128)(2,1)S(1)}, f32[2048,1024]{1,0:T(8,128)S(1)}, f32[16,256]{1,0:T(8,128)S(1)}, f32[16,256]{1,0:T(8,128)S(1)}) custom-call(bf16[512,2048]{1,0:T(8,128)(2,1)} %acts.1, bf16[512,1024]{1,0:T(8,128)(2,1)} %grads.1, bf16[2048,512]{1,0:T(8,128)(2,1)} %proj.1, ...), custom_call_target="tpu_custom_call" | custom-call | tf_op jit(solution)/shard_map/pallas_call | solution.py:245
  32.1 5.2 %shard_map.94 = (f32[2048,1024]{1,0:T(8,128)}, bf16[2048,1024]{1,0:T(8,128)(2,1)}, f32[16,256]{1,0:T(8,128)}, f32[16,256]{1,0:T(8,128)}) custom-call(bf16[2,2,2,2,2,2,2,2,16,128]{9,8,7,6,5,4,3,2,1,0:T(8,128)(2,1)S(1)} %get-tuple-element.9.gathered, bf16[2048,512]{1,0:T(8,128)(2,1)S(1)} %get-tuple-element.10.proj, f32[2048,1024]{1,0:T(8,128)S(1)} %get-tuple-element.11.weight, ...), custom_call_target="tpu_custom_call" | custom-call | tf_op jit(solution)/shard_map/pallas_call | solution.py:346

commit v5 on v4

--- a/solution.py
+++ b/solution.py
@@ -26,6 +26,7 @@
 
 
 MASKS = (7, 6, 5, 3, 4, 2, 1)
+PIECES = ((0, 0), (0, 1), (1, 0), (1, 1))
 
 
 def bits(m):
@@ -130,14 +131,19 @@
         started.append(copy)
         return copy
 
-    def spread(stage, half, flips, source, target=None):
+    def spread(stage, piece, half, flips, source, target=None):
         copies = []
         for n, m in enumerate(MASKS):
             src = source(m)
             dst = src if target is None else target(n)
             device = partner((half == 1) == (flips == 1), m)
-            copies.append(send(src, dst, send_sem.at[stage, half, n], recv_sem.at[stage, half, n], device))
+            at = (stage, piece, half, n)
+            copies.append(send(src, dst, send_sem.at[at], recv_sem.at[at], device))
         return copies
+
+    def arrived(copies):
+        for copy in copies:
+            copy.wait_recv()
 
     load_proj.wait()
     pair = []
@@ -153,7 +159,7 @@
     for copy in load_moments:
         copy.wait()
     gather0 = [
-        spread(0, half, 2, lambda m, half=half: moments.at[(half, *members[half])]) for half in range(2)
+        spread(0, 0, half, 2, lambda m, half=half: moments.at[(half, *members[half])]) for half in range(2)
     ]
     for copy in load_grads:
         copy.wait()
@@ -163,7 +169,18 @@
         pair[t].wait_recv()
         both[:, t * chunk : (t + 1) * chunk] = (summed[rows, :] + theirs[rows, :].astype(F32)).T.astype(BF16)
 
-    stage1 = []
+    stage1, stage2, gather2 = {}, {}, {}
+
+    def scatter(piece, half):
+        stage1[piece, half] = spread(
+            1,
+            piece,
+            half,
+            1,
+            lambda m: parts.at[(half, *flip(sets[half], m), piece)],
+            lambda n: got1.at[half, piece, n],
+        )
+
     for half in range(2):
         block = jnp.dot(both[...], grads_v[half], preferred_element_type=F32).astype(BF16)
         for x in range(4):
@@ -173,67 +190,51 @@
                     at = [place(half, v) for v in (x, y, z)]
                     index = tuple(p[0] for p in at) + tuple(p[1] for p in at)
                     parts[(half, *index)] = block[row : row + 16, column : column + 128]
-        stage1.append(
-            spread(
-                1,
-                half,
-                1,
-                lambda m: parts.at[(half, *flip(sets[half], m))],
-                lambda n: got1.at[half, n],
-            )
-        )
-
-    stage2 = []
-    for half in range(2):
-        for copy in stage1[half]:
-            copy.wait_recv()
-        total = parts[(half, *sets[half])].astype(F32)
+        scatter(0, half)
+    scatter(1, 0)
+    scatter(1, 1)
+
+    for piece, half in PIECES:
+        arrived(stage1[piece, half])
+        total = parts[(half, *sets[half], piece)].astype(F32)
         for n in range(7):
-            total += got1[half, n].astype(F32)
-        own = (half, *members[half])
+            total += got1[half, piece, n].astype(F32)
+        own = (half, *members[half], piece)
         sums[own] = total.astype(BF16)
-        stage2.append(spread(2, half, 2, lambda m: sums.at[own]))
-
-    gather2 = []
-    for half in range(2):
-        for copy in gather0[half]:
-            copy.wait_recv()
-        for copy in stage2[half]:
-            copy.wait_recv()
-        for i in range(2):
-            for j in range(2):
-                for k in range(2):
-                    coefficients = sums[half, 0, 0, 0, i, j, k].astype(F32)
-                    for n in range(1, 8):
-                        coefficients += sums[(half, *bits(n), i, j, k)].astype(F32)
-                    first_new = first_decay * moments[half, i, j, k, 0] + (1.0 - first_decay) * coefficients
-                    second_new = (
-                        second_decay * moments[half, i, j, k, 1]
-                        + (1.0 - second_decay) * coefficients * coefficients
-                    )
-                    normalized = first_new / first_bias / (jnp.sqrt(second_new / second_bias) + epsilon)
-                    gathered[(c, half, *sets[half], i, j, k)] = normalized.astype(BF16)
-                    states[half, i, j, k, 0] = first_new
-                    states[half, i, j, k, 1] = second_new
-        gather2.append(spread(3, half, 1, lambda m: gathered.at[(c, half, *sets[half])]))
+        stage2[piece, half] = spread(2, piece, half, 2, lambda m: sums.at[own])
+
+    for piece, half in PIECES:
+        if piece == 0:
+            arrived(gather0[half])
+        arrived(stage2[piece, half])
+        for j in range(2):
+            for k in range(2):
+                coefficients = sums[half, 0, 0, 0, piece, j, k].astype(F32)
+                for n in range(1, 8):
+                    coefficients += sums[(half, *bits(n), piece, j, k)].astype(F32)
+                first_new = first_decay * moments[half, piece, j, k, 0] + (1.0 - first_decay) * coefficients
+                second_new = (
+                    second_decay * moments[half, piece, j, k, 1]
+                    + (1.0 - second_decay) * coefficients * coefficients
+                )
+                normalized = first_new / first_bias / (jnp.sqrt(second_new / second_bias) + epsilon)
+                gathered[(c, half, *sets[half], piece, j, k)] = normalized.astype(BF16)
+                states[half, piece, j, k, 0] = first_new
+                states[half, piece, j, k, 1] = second_new
+        gather2[piece, half] = spread(3, piece, half, 1, lambda m: gathered.at[(c, half, *sets[half], piece)])
     for half in range(2):
         columns = slice(half * 128, (half + 1) * 128)
         first_new_ref[:, columns] = states[(half, *members[half], 0)]
         second_new_ref[:, columns] = states[(half, *members[half], 1)]
 
     forwards = []
-    for far in range(2):
-        for half in range(2):
-            for n, m in enumerate(MASKS):
-                if m // 4 == far:
-                    gather2[half][n].wait_recv()
-            x = sets[half][0]
-            block = gathered.at[c, half, 1 - x if far else x]
-            forwards.append(send(block, block, fw_send.at[half, far], fw_recv.at[half, far], sibling))
-    for copy in forwards:
-        copy.wait_recv()
+    for piece, half in PIECES:
+        arrived(gather2[piece, half])
+        block = gathered.at[c, half, :, :, :, piece]
+        forwards.append(send(block, block, fw_send.at[half, piece], fw_recv.at[half, piece], sibling))
     for copy in started:
         copy.wait_send()
+    arrived(forwards)
     load_weight.wait()
 
 
@@ -261,15 +262,15 @@
             pltpu.VMEM((512, 512), BF16),
             pltpu.VMEM((512, 512), F32),
             pltpu.VMEM((2, 2, 2, 2, 2, 2, 2, 16, 128), BF16),
-            pltpu.VMEM((2, 7, 2, 2, 2, 16, 128), BF16),
+            pltpu.VMEM((2, 2, 7, 2, 2, 16, 128), BF16),
             pltpu.VMEM((2, 2, 2, 2, 2, 2, 2, 16, 128), BF16),
             pltpu.VMEM((2, 2, 2, 2, 2, 16, 128), F32),
             pltpu.VMEM((2, 2, 2, 2, 2, 16, 128), F32),
             dma((10 + TOKEN_CHUNKS,)),
             dma((TOKEN_CHUNKS,)),
             dma((TOKEN_CHUNKS,)),
-            dma((4, 2, 7)),
-            dma((4, 2, 7)),
+            dma((4, 2, 2, 7)),
+            dma((4, 2, 2, 7)),
             dma((2, 2)),
             dma((2, 2)),
         ],

time: 37.5 us -> 37.8 us (level)
  Pallas kernels: 36.7 us -> 37.1 us
where the time goes in v5:
time: 37.8 us; the launch traced here: 37.7 us
  Pallas kernels  37.1 us (98%)
  between operations  0.64 us (2%)
    pallas_call x1, Pallas kernels, reduce_and_gather(): pl.pallas_call(reduce_kernel, out_shape=(pltpu.VMEM((2, 2, 2, 2, 2, 2, 2,...  31.8 us
    pallas_call x1, Pallas kernels, expand(): pl.pallas_call(expand_kernel, out_shape=(jax.ShapeDtypeStruct((depth, 102...  5.23 us

profile of v5, /device:TPU:1, one launch (start us, length us, event | category | flops | bytes accessed | tf_op | source)
XLA Modules:
  0.0 37.7 jit_solution(9194136786247745662)
XLA Ops:
  0.6 31.8 %shard_map.93 = (bf16[2,2,2,2,2,2,2,2,16,128]{9,8,7,6,5,4,3,2,1,0:T(8,128)(2,1)S(1)}, bf16[2048,512]{1,0:T(8,128)(2,1)S(1)}, f32[2048,1024]{1,0:T(8,128)S(1)}, f32[16,256]{1,0:T(8,128)S(1)}, f32[16,256]{1,0:T(8,128)S(1)}) custom-call(bf16[512,2048]{1,0:T(8,128)(2,1)} %acts.1, bf16[512,1024]{1,0:T(8,128)(2,1)} %grads.1, bf16[2048,512]{1,0:T(8,128)(2,1)} %proj.1, ...), custom_call_target="tpu_custom_call" | custom-call | tf_op jit(solution)/shard_map/pallas_call | solution.py:246
  32.5 5.2 %shard_map.94 = (f32[2048,1024]{1,0:T(8,128)}, bf16[2048,1024]{1,0:T(8,128)(2,1)}, f32[16,256]{1,0:T(8,128)}, f32[16,256]{1,0:T(8,128)}) custom-call(bf16[2,2,2,2,2,2,2,2,16,128]{9,8,7,6,5,4,3,2,1,0:T(8,128)(2,1)S(1)} %get-tuple-element.9.gathered, bf16[2048,512]{1,0:T(8,128)(2,1)S(1)} %get-tuple-element.10.proj, f32[2048,1024]{1,0:T(8,128)S(1)} %get-tuple-element.11.weight, ...), custom_call_target="tpu_custom_call" | custom-call | tf_op jit(solution)/shard_map/pallas_call | solution.py:347

commit v6 on v4

--- a/solution.py
+++ b/solution.py
@@ -18,11 +18,16 @@
 F32 = jnp.float32
 BF16 = jnp.bfloat16
 TOKEN_CHUNKS = 4
+DEPTH_CHUNKS = 4
 ROW_TILE = 256
 
 
-def place(half, v):
-    return ((v + v // 2) % 2, v // 2) if half == 0 else (v // 2, v % 2)
+WRAP_FIRST = ((False, False, True), (True, True, False))
+HALVES = (1, 0)
+
+
+def place(wrap_first, v):
+    return (v // 2, v % 2) if wrap_first else ((v + v // 2) % 2, v // 2)
 
 
 MASKS = (7, 6, 5, 3, 4, 2, 1)
@@ -69,29 +74,48 @@
     chip = (dp // 8, (dp // 2) % 4, zh * 2 + dp % 2)
     sibling = (dp, zh * 2 + 1 - c)
 
-    def partner(wrap, m):
-        x, y, z = ((3 - v if wrap else v + 1 - 2 * (v % 2)) if bit else v for v, bit in zip(chip, bits(m)))
-        return (x * 8 + y * 2 + z % 2, (z // 2) * 2 + c)
+    terms = []
+    for axis, v in enumerate(chip):
+        options = (v, v + 1 - 2 * (v % 2), 3 - v)
+        if axis == 2:
+            terms.append([(o % 2, o // 2 * 2 + c) for o in options])
+        else:
+            terms.append([(o * (8, 2)[axis], 0) for o in options])
+
+    def partner(half, flips, m):
+        x, y, z = (
+            terms[axis][(2 if WRAP_FIRST[half][axis] == (flips == 1) else 1) if bit else 0]
+            for axis, bit in enumerate(bits(m))
+        )
+        return (x[0] + y[0] + z[0], z[1])
 
     def flip(at, m):
         return tuple(1 - v if bit else v for v, bit in zip(at, bits(m)))
 
     sets, members = [], []
     for half in range(2):
-        places = [place(half, v) for v in chip]
+        places = [place(w, v) for w, v in zip(WRAP_FIRST[half], chip)]
         sets.append(tuple(p[0] for p in places))
         members.append(tuple(p[1] for p in places))
 
     tokens = acts.shape[0]
     chunk = tokens // TOKEN_CHUNKS
-    load_proj = pltpu.make_async_copy(proj, proj_v, load_sem.at[0])
-    load_proj.start()
-    load_acts = []
-    for t in range(TOKEN_CHUNKS):
+    depth = proj.shape[0] // DEPTH_CHUNKS
+    load_proj, load_acts = [], []
+
+    def load(loads, src, dst):
+        copy = pltpu.make_async_copy(src, dst, load_sem.at[len(load_proj) + len(load_acts)])
+        copy.start()
+        loads.append(copy)
+
+    for k in range(DEPTH_CHUNKS):
+        rows = pl.ds(k * depth, depth)
+        load(load_proj, proj.at[rows], proj_v.at[rows])
+        if k == 0:
+            load(load_acts, acts.at[pl.ds(0, chunk)], acts_v.at[pl.ds(0, chunk)])
+    for t in range(1, TOKEN_CHUNKS):
         rows = pl.ds(t * chunk, chunk)
-        copy = pltpu.make_async_copy(acts.at[rows], acts_v.at[rows], load_sem.at[1 + t])
-        copy.start()
-        load_acts.append(copy)
+        load(load_acts, acts.at[rows], acts_v.at[rows])
     load_grads = []
     for half in range(2):
         for h in range(2):
@@ -99,7 +123,7 @@
             copy = pltpu.make_async_copy(
                 grads.at[:, columns],
                 grads_v.at[half, :, pl.ds(h * 128, 128)],
-                load_sem.at[1 + TOKEN_CHUNKS + 2 * half + h],
+                load_sem.at[DEPTH_CHUNKS + TOKEN_CHUNKS + 2 * half + h],
             )
             copy.start()
             load_grads.append(copy)
@@ -110,14 +134,14 @@
             copy = pltpu.make_async_copy(
                 moment.at[:, columns],
                 moments.at[(half, *members[half], n)],
-                load_sem.at[5 + TOKEN_CHUNKS + 2 * half + n],
+                load_sem.at[4 + DEPTH_CHUNKS + TOKEN_CHUNKS + 2 * half + n],
             )
             copy.start()
             load_moments.append(copy)
-    load_weight = pltpu.make_async_copy(weight, weight_v, load_sem.at[9 + TOKEN_CHUNKS])
+    load_weight = pltpu.make_async_copy(weight, weight_v, load_sem.at[8 + DEPTH_CHUNKS + TOKEN_CHUNKS])
 
     barrier = pltpu.get_barrier_semaphore()
-    for device in [sibling] + [partner(wrap, m) for wrap in (False, True) for m in MASKS]:
+    for device in [sibling] + [partner(0, flips, m) for flips in (1, 2) for m in MASKS]:
         pl.semaphore_signal(barrier, inc=1, device_id=device, device_id_type=MESH)
 
     started = []
@@ -135,16 +159,22 @@
         for n, m in enumerate(MASKS):
             src = source(m)
             dst = src if target is None else target(n)
-            device = partner((half == 1) == (flips == 1), m)
+            device = partner(half, flips, m)
             copies.append(send(src, dst, send_sem.at[stage, half, n], recv_sem.at[stage, half, n], device))
         return copies
 
-    load_proj.wait()
     pair = []
     for t in range(TOKEN_CHUNKS):
         rows = pl.ds(t * chunk, chunk)
         load_acts[t].wait()
-        projected = jnp.dot(acts_v[rows, :], proj_v[...], preferred_element_type=F32)
+        if t == 0:
+            projected = jnp.zeros((chunk, proj.shape[1]), F32)
+            for k in range(DEPTH_CHUNKS):
+                at = pl.ds(k * depth, depth)
+                load_proj[k].wait()
+                projected += jnp.dot(acts_v[rows, at], proj_v[at, :], preferred_element_type=F32)
+        else:
+            projected = jnp.dot(acts_v[rows, :], proj_v[...], preferred_element_type=F32)
         mine[rows, :] = projected.astype(BF16)
         summed[rows, :] = projected
         if t == 0:
@@ -152,9 +182,9 @@
         pair.append(send(mine.at[rows], theirs.at[rows], pair_send.at[t], pair_recv.at[t], sibling))
     for copy in load_moments:
         copy.wait()
-    gather0 = [
-        spread(0, half, 2, lambda m, half=half: moments.at[(half, *members[half])]) for half in range(2)
-    ]
+    gather0 = {}
+    for half in HALVES:
+        gather0[half] = spread(0, half, 2, lambda m: moments.at[(half, *members[half])])
     for copy in load_grads:
         copy.wait()
     load_weight.start()
@@ -163,28 +193,21 @@
         pair[t].wait_recv()
         both[:, t * chunk : (t + 1) * chunk] = (summed[rows, :] + theirs[rows, :].astype(F32)).T.astype(BF16)
 
-    stage1 = []
-    for half in range(2):
+    stage1, stage2, gather2 = {}, {}, {}
+    for half in HALVES:
         block = jnp.dot(both[...], grads_v[half], preferred_element_type=F32).astype(BF16)
         for x in range(4):
             for y in range(4):
                 for z in range(4):
                     row, column = x * 128 + y * 32 + z % 2 * 16, z // 2 * 128
-                    at = [place(half, v) for v in (x, y, z)]
+                    at = [place(w, v) for w, v in zip(WRAP_FIRST[half], (x, y, z))]
                     index = tuple(p[0] for p in at) + tuple(p[1] for p in at)
                     parts[(half, *index)] = block[row : row + 16, column : column + 128]
-        stage1.append(
-            spread(
-                1,
-                half,
-                1,
-                lambda m: parts.at[(half, *flip(sets[half], m))],
-                lambda n: got1.at[half, n],
-            )
+        stage1[half] = spread(
+            1, half, 1, lambda m: parts.at[(half, *flip(sets[half], m))], lambda n: got1.at[half, n]
         )
 
-    stage2 = []
-    for half in range(2):
+    for half in HALVES:
         for copy in stage1[half]:
             copy.wait_recv()
         total = parts[(half, *sets[half])].astype(F32)
@@ -192,10 +215,9 @@
             total += got1[half, n].astype(F32)
         own = (half, *members[half])
         sums[own] = total.astype(BF16)
-        stage2.append(spread(2, half, 2, lambda m: sums.at[own]))
-
-    gather2 = []
-    for half in range(2):
+        stage2[half] = spread(2, half, 2, lambda m: sums.at[own])
+
+    for half in HALVES:
         for copy in gather0[half]:
             copy.wait_recv()
         for copy in stage2[half]:
@@ -215,26 +237,23 @@
                     gathered[(c, half, *sets[half], i, j, k)] = normalized.astype(BF16)
                     states[half, i, j, k, 0] = first_new
                     states[half, i, j, k, 1] = second_new
-        gather2.append(spread(3, half, 1, lambda m: gathered.at[(c, half, *sets[half])]))
+        gather2[half] = spread(3, half, 1, lambda m: gathered.at[(c, half, *sets[half])])
     for half in range(2):
         columns = slice(half * 128, (half + 1) * 128)
         first_new_ref[:, columns] = states[(half, *members[half], 0)]
         second_new_ref[:, columns] = states[(half, *members[half], 1)]
 
+    load_weight.wait()
     forwards = []
-    for far in range(2):
-        for half in range(2):
-            for n, m in enumerate(MASKS):
-                if m // 4 == far:
-                    gather2[half][n].wait_recv()
-            x = sets[half][0]
-            block = gathered.at[c, half, 1 - x if far else x]
-            forwards.append(send(block, block, fw_send.at[half, far], fw_recv.at[half, far], sibling))
+    for half in HALVES:
+        for copy in gather2[half]:
+            copy.wait_recv()
+        block = gathered.at[c, half]
+        forwards.append(send(block, block, fw_send.at[half], fw_recv.at[half], sibling))
+    for copy in started:
+        copy.wait_send()
     for copy in forwards:
         copy.wait_recv()
-    for copy in started:
-        copy.wait_send()
-    load_weight.wait()
 
 
 def reduce_and_gather(*operands):
@@ -265,13 +284,13 @@
             pltpu.VMEM((2, 2, 2, 2, 2, 2, 2, 16, 128), BF16),
             pltpu.VMEM((2, 2, 2, 2, 2, 16, 128), F32),
             pltpu.VMEM((2, 2, 2, 2, 2, 16, 128), F32),
-            dma((10 + TOKEN_CHUNKS,)),
+            dma((9 + DEPTH_CHUNKS + TOKEN_CHUNKS,)),
             dma((TOKEN_CHUNKS,)),
             dma((TOKEN_CHUNKS,)),
             dma((4, 2, 7)),
             dma((4, 2, 7)),
-            dma((2, 2)),
-            dma((2, 2)),
+            dma((2,)),
+            dma((2,)),
         ],
         compiler_params=pltpu.CompilerParams(
             collective_id=0, has_side_effects=True, vmem_limit_bytes=24 * 1024 * 1024
@@ -316,7 +335,7 @@
                 for x in range(4):
                     for y in range(4):
                         for zl in range(2):
-                            at = [place(half, v) for v in (x, y, zh * 2 + zl)]
+                            at = [place(w, v) for w, v in zip(WRAP_FIRST[half], (x, y, zh * 2 + zl))]
                             index = tuple(p[0] for p in at) + tuple(p[1] for p in at)
                             row = x * 128 + y * 32 + zl * 16
                             ordered[row : row + 16, column : column + 128] = gathered[(c, half, *index)]

time: 37.5 us -> 36.4 us (0.971)
  Pallas kernels: 36.7 us -> 35.7 us
    pallas_call x1, Pallas kernels: 31.5 us -> 30.4 us  [reduce_and_gather(): pl.pallas_call(reduce_kernel, out_shape=(pltpu.VMEM((2, 2, 2, 2, 2, 2, 2,...]
where the time goes in v6:
time: 36.4 us; the launch traced here: 36.3 us
  Pallas kernels  35.7 us (98%)
  between operations  0.64 us (2%)
    pallas_call x1, Pallas kernels, reduce_and_gather(): pl.pallas_call(reduce_kernel, out_shape=(pltpu.VMEM((2, 2, 2, 2, 2, 2, 2,...  30.4 us
    pallas_call x1, Pallas kernels, expand(): pl.pallas_call(expand_kernel, out_shape=(jax.ShapeDtypeStruct((depth, 102...  5.24 us

profile of v6, /device:TPU:1, one launch (start us, length us, event | category | flops | bytes accessed | tf_op | source)
XLA Modules:
  0.0 36.3 jit_solution(11556518482437572781)
XLA Ops:
  0.6 30.4 %shard_map.93 = (bf16[2,2,2,2,2,2,2,2,16,128]{9,8,7,6,5,4,3,2,1,0:T(8,128)(2,1)S(1)}, bf16[2048,512]{1,0:T(8,128)(2,1)S(1)}, f32[2048,1024]{1,0:T(8,128)S(1)}, f32[16,256]{1,0:T(8,128)S(1)}, f32[16,256]{1,0:T(8,128)S(1)}) custom-call(bf16[512,2048]{1,0:T(8,128)(2,1)} %acts.1, bf16[512,1024]{1,0:T(8,128)(2,1)} %grads.1, bf16[2048,512]{1,0:T(8,128)(2,1)} %proj.1, ...), custom_call_target="tpu_custom_call" | custom-call | tf_op jit(solution)/shard_map/pallas_call | solution.py:264
  31.1 5.2 %shard_map.94 = (f32[2048,1024]{1,0:T(8,128)}, bf16[2048,1024]{1,0:T(8,128)(2,1)}, f32[16,256]{1,0:T(8,128)}, f32[16,256]{1,0:T(8,128)}) custom-call(bf16[2,2,2,2,2,2,2,2,16,128]{9,8,7,6,5,4,3,2,1,0:T(8,128)(2,1)S(1)} %get-tuple-element.9.gathered, bf16[2048,512]{1,0:T(8,128)(2,1)S(1)} %get-tuple-element.10.proj, f32[2048,1024]{1,0:T(8,128)S(1)} %get-tuple-element.11.weight, ...), custom_call_target="tpu_custom_call" | custom-call | tf_op jit(solution)/shard_map/pallas_call | solution.py:365

commit v7 on v6

--- a/solution.py
+++ b/solution.py
@@ -17,8 +17,8 @@
 MESH = pl.DeviceIdType.MESH
 F32 = jnp.float32
 BF16 = jnp.bfloat16
-TOKEN_CHUNKS = 4
-DEPTH_CHUNKS = 4
+TOKEN_BLOCKS = 4
+DEPTH_PARTS = 8
 ROW_TILE = 256
 
 
@@ -98,24 +98,22 @@
         sets.append(tuple(p[0] for p in places))
         members.append(tuple(p[1] for p in places))
 
-    tokens = acts.shape[0]
-    chunk = tokens // TOKEN_CHUNKS
-    depth = proj.shape[0] // DEPTH_CHUNKS
-    load_proj, load_acts = [], []
-
-    def load(loads, src, dst):
-        copy = pltpu.make_async_copy(src, dst, load_sem.at[len(load_proj) + len(load_acts)])
-        copy.start()
-        loads.append(copy)
-
-    for k in range(DEPTH_CHUNKS):
-        rows = pl.ds(k * depth, depth)
-        load(load_proj, proj.at[rows], proj_v.at[rows])
-        if k == 0:
-            load(load_acts, acts.at[pl.ds(0, chunk)], acts_v.at[pl.ds(0, chunk)])
-    for t in range(1, TOKEN_CHUNKS):
-        rows = pl.ds(t * chunk, chunk)
-        load(load_acts, acts.at[rows], acts_v.at[rows])
+    depth = proj.shape[0] // DEPTH_PARTS
+    load_parts = []
+
+    def load_part(k):
+        at = pl.ds(k * depth, depth)
+        for n, (src, dst) in enumerate(((proj.at[at], proj_v.at[at]), (acts.at[:, at], acts_v.at[:, at]))):
+            copy = pltpu.make_async_copy(src, dst, load_sem.at[2 * k + n])
+            copy.start()
+            load_parts.append(copy)
+
+    load_part(0)
+    barrier = pltpu.get_barrier_semaphore()
+    for device in [sibling] + [partner(0, flips, m) for flips in (1, 2) for m in MASKS]:
+        pl.semaphore_signal(barrier, inc=1, device_id=device, device_id_type=MESH)
+    for k in range(1, DEPTH_PARTS):
+        load_part(k)
     load_grads = []
     for half in range(2):
         for h in range(2):
@@ -123,7 +121,7 @@
             copy = pltpu.make_async_copy(
                 grads.at[:, columns],
                 grads_v.at[half, :, pl.ds(h * 128, 128)],
-                load_sem.at[DEPTH_CHUNKS + TOKEN_CHUNKS + 2 * half + h],
+                load_sem.at[2 * DEPTH_PARTS + 2 * half + h],
             )
             copy.start()
             load_grads.append(copy)
@@ -134,15 +132,11 @@
             copy = pltpu.make_async_copy(
                 moment.at[:, columns],
                 moments.at[(half, *members[half], n)],
-                load_sem.at[4 + DEPTH_CHUNKS + TOKEN_CHUNKS + 2 * half + n],
+                load_sem.at[4 + 2 * DEPTH_PARTS + 2 * half + n],
             )
             copy.start()
             load_moments.append(copy)
-    load_weight = pltpu.make_async_copy(weight, weight_v, load_sem.at[8 + DEPTH_CHUNKS + TOKEN_CHUNKS])
-
-    barrier = pltpu.get_barrier_semaphore()
-    for device in [sibling] + [partner(0, flips, m) for flips in (1, 2) for m in MASKS]:
-        pl.semaphore_signal(barrier, inc=1, device_id=device, device_id_type=MESH)
+    load_weight = pltpu.make_async_copy(weight, weight_v, load_sem.at[8 + 2 * DEPTH_PARTS])
 
     started = []
 
@@ -163,49 +157,45 @@
             copies.append(send(src, dst, send_sem.at[stage, half, n], recv_sem.at[stage, half, n], device))
         return copies
 
-    pair = []
-    for t in range(TOKEN_CHUNKS):
-        rows = pl.ds(t * chunk, chunk)
-        load_acts[t].wait()
-        if t == 0:
-            projected = jnp.zeros((chunk, proj.shape[1]), F32)
-            for k in range(DEPTH_CHUNKS):
-                at = pl.ds(k * depth, depth)
-                load_proj[k].wait()
-                projected += jnp.dot(acts_v[rows, at], proj_v[at, :], preferred_element_type=F32)
-        else:
-            projected = jnp.dot(acts_v[rows, :], proj_v[...], preferred_element_type=F32)
-        mine[rows, :] = projected.astype(BF16)
-        summed[rows, :] = projected
-        if t == 0:
-            pl.semaphore_wait(barrier, 15)
-        pair.append(send(mine.at[rows], theirs.at[rows], pair_send.at[t], pair_recv.at[t], sibling))
-    for copy in load_moments:
-        copy.wait()
-    gather0 = {}
-    for half in HALVES:
-        gather0[half] = spread(0, half, 2, lambda m: moments.at[(half, *members[half])])
+    for k in range(DEPTH_PARTS):
+        at = pl.ds(k * depth, depth)
+        load_parts[2 * k].wait()
+        load_parts[2 * k + 1].wait()
+        product = jnp.dot(acts_v[:, at], proj_v[at, :], preferred_element_type=F32)
+        projected = product if k == 0 else projected + product
+    block = projected.shape[0] // TOKEN_BLOCKS
+    for t in range(TOKEN_BLOCKS):
+        turned = projected[t * block : (t + 1) * block].T
+        summed[t] = turned
+        mine[t] = turned.astype(BF16)
+    pl.semaphore_wait(barrier, 15)
+    pair = [send(mine.at[t], theirs.at[t], pair_send.at[t], pair_recv.at[t], sibling) for t in range(TOKEN_BLOCKS)]
     for copy in load_grads:
         copy.wait()
     load_weight.start()
-    for t in range(TOKEN_CHUNKS):
-        rows = pl.ds(t * chunk, chunk)
+    for t in range(TOKEN_BLOCKS):
         pair[t].wait_recv()
-        both[:, t * chunk : (t + 1) * chunk] = (summed[rows, :] + theirs[rows, :].astype(F32)).T.astype(BF16)
+        both[:, t * block : (t + 1) * block] = (summed[t] + theirs[t].astype(F32)).astype(BF16)
 
     stage1, stage2, gather2 = {}, {}, {}
     for half in HALVES:
-        block = jnp.dot(both[...], grads_v[half], preferred_element_type=F32).astype(BF16)
+        product = jnp.dot(both[...], grads_v[half], preferred_element_type=F32).astype(BF16)
         for x in range(4):
             for y in range(4):
                 for z in range(4):
                     row, column = x * 128 + y * 32 + z % 2 * 16, z // 2 * 128
                     at = [place(w, v) for w, v in zip(WRAP_FIRST[half], (x, y, z))]
                     index = tuple(p[0] for p in at) + tuple(p[1] for p in at)
-                    parts[(half, *index)] = block[row : row + 16, column : column + 128]
+                    parts[(half, *index)] = product[row : row + 16, column : column + 128]
         stage1[half] = spread(
             1, half, 1, lambda m: parts.at[(half, *flip(sets[half], m))], lambda n: got1.at[half, n]
         )
+
+    for copy in load_moments:
+        copy.wait()
+    gather0 = {}
+    for half in HALVES:
+        gather0[half] = spread(0, half, 2, lambda m: moments.at[(half, *members[half])])
 
     for half in HALVES:
         for copy in stage1[half]:
@@ -275,18 +265,18 @@
         scratch_shapes=[
             pltpu.VMEM((512, 2048), BF16),
             pltpu.VMEM((2, 512, 256), BF16),
+            pltpu.VMEM((TOKEN_BLOCKS, 512, 512 // TOKEN_BLOCKS), BF16),
+            pltpu.VMEM((TOKEN_BLOCKS, 512, 512 // TOKEN_BLOCKS), BF16),
             pltpu.VMEM((512, 512), BF16),
-            pltpu.VMEM((512, 512), BF16),
-            pltpu.VMEM((512, 512), BF16),
-            pltpu.VMEM((512, 512), F32),
+            pltpu.VMEM((TOKEN_BLOCKS, 512, 512 // TOKEN_BLOCKS), F32),
             pltpu.VMEM((2, 2, 2, 2, 2, 2, 2, 16, 128), BF16),
             pltpu.VMEM((2, 7, 2, 2, 2, 16, 128), BF16),
             pltpu.VMEM((2, 2, 2, 2, 2, 2, 2, 16, 128), BF16),
             pltpu.VMEM((2, 2, 2, 2, 2, 16, 128), F32),
             pltpu.VMEM((2, 2, 2, 2, 2, 16, 128), F32),
-            dma((9 + DEPTH_CHUNKS + TOKEN_CHUNKS,)),
-            dma((TOKEN_CHUNKS,)),
-            dma((TOKEN_CHUNKS,)),
+            dma((9 + 2 * DEPTH_PARTS,)),
+            dma((TOKEN_BLOCKS,)),
+            dma((TOKEN_BLOCKS,)),
             dma((4, 2, 7)),
             dma((4, 2, 7)),
             dma((2,)),

time: 36.4 us -> 36.7 us (level)
  no operation moved by 1% of the time
where the time goes in v7:
time: 36.7 us; the launch traced here: 36.5 us
  Pallas kernels  35.9 us (98%)
  between operations  0.64 us (2%)
    pallas_call x1, Pallas kernels, reduce_and_gather(): pl.pallas_call(reduce_kernel, out_shape=(pltpu.VMEM((2, 2, 2, 2, 2, 2, 2,...  30.7 us
    pallas_call x1, Pallas kernels, expand(): pl.pallas_call(expand_kernel, out_shape=(jax.ShapeDtypeStruct((depth, 102...  5.23 us

profile of v7, /device:TPU:1, one launch (start us, length us, event | category | flops | bytes accessed | tf_op | source)
XLA Modules:
  0.0 36.5 jit_solution(10270523255953476966)
XLA Ops:
  0.6 30.7 %shard_map.93 = (bf16[2,2,2,2,2,2,2,2,16,128]{9,8,7,6,5,4,3,2,1,0:T(8,128)(2,1)S(1)}, bf16[2048,512]{1,0:T(8,128)(2,1)S(1)}, f32[2048,1024]{1,0:T(8,128)S(1)}, f32[16,256]{1,0:T(8,128)S(1)}, f32[16,256]{1,0:T(8,128)S(1)}) custom-call(bf16[512,2048]{1,0:T(8,128)(2,1)} %acts.1, bf16[512,1024]{1,0:T(8,128)(2,1)} %grads.1, bf16[2048,512]{1,0:T(8,128)(2,1)} %proj.1, ...), custom_call_target="tpu_custom_call" | custom-call | tf_op jit(solution)/shard_map/pallas_call | solution.py:254
  31.3 5.2 %shard_map.94 = (f32[2048,1024]{1,0:T(8,128)}, bf16[2048,1024]{1,0:T(8,128)(2,1)}, f32[16,256]{1,0:T(8,128)}, f32[16,256]{1,0:T(8,128)}) custom-call(bf16[2,2,2,2,2,2,2,2,16,128]{9,8,7,6,5,4,3,2,1,0:T(8,128)(2,1)S(1)} %get-tuple-element.9.gathered, bf16[2048,512]{1,0:T(8,128)(2,1)S(1)} %get-tuple-element.10.proj, f32[2048,1024]{1,0:T(8,128)S(1)} %get-tuple-element.11.weight, ...), custom_call_target="tpu_custom_call" | custom-call | tf_op jit(solution)/shard_map/pallas_call | solution.py:355

commit v8 on v7

--- a/solution.py
+++ b/solution.py
@@ -19,7 +19,7 @@
 BF16 = jnp.bfloat16
 TOKEN_BLOCKS = 4
 DEPTH_PARTS = 8
-ROW_TILE = 256
+ROW_TILE = 512
 
 
 WRAP_FIRST = ((False, False, True), (True, True, False))
@@ -44,11 +44,15 @@
     weight,
     first_moment,
     second_moment,
-    gathered,
+    other,
+    own_new,
+    own_update,
     proj_v,
     weight_v,
     first_new_ref,
     second_new_ref,
+    gathered,
+    own,
     acts_v,
     grads_v,
     mine,
@@ -203,9 +207,9 @@
         total = parts[(half, *sets[half])].astype(F32)
         for n in range(7):
             total += got1[half, n].astype(F32)
-        own = (half, *members[half])
-        sums[own] = total.astype(BF16)
-        stage2[half] = spread(2, half, 2, lambda m: sums.at[own])
+        here = (half, *members[half])
+        sums[here] = total.astype(BF16)
+        stage2[half] = spread(2, half, 2, lambda m: sums.at[here])
 
     for half in HALVES:
         for copy in gather0[half]:
@@ -233,17 +237,42 @@
         first_new_ref[:, columns] = states[(half, *members[half], 0)]
         second_new_ref[:, columns] = states[(half, *members[half], 1)]
 
-    load_weight.wait()
-    forwards = []
+    forwards = {}
     for half in HALVES:
         for copy in gather2[half]:
             copy.wait_recv()
         block = gathered.at[c, half]
-        forwards.append(send(block, block, fw_send.at[half], fw_recv.at[half], sibling))
+        forwards[half] = send(block, block, fw_send.at[half], fw_recv.at[half], sibling)
+
+    def order(core, half, target):
+        for x in range(4):
+            for y in range(4):
+                for z in range(4):
+                    row, column = x * 128 + y * 32 + z % 2 * 16, z // 2 * 256 + half * 128
+                    at = [place(w, v) for w, v in zip(WRAP_FIRST[half], (x, y, z))]
+                    index = tuple(p[0] for p in at) + tuple(p[1] for p in at)
+                    target[row : row + 16, column : column + 128] = gathered[(core, half, *index)]
+
+    for half in HALVES:
+        order(c, half, own)
+    load_weight.wait()
+    for rows, columns, here in column_tiles(weight_v.shape[0], c):
+        expanded = jnp.dot(proj_v[rows, :], own[:, columns], preferred_element_type=F32)
+        own_new[rows, columns] = weight_v[rows, here] - step_rate * expanded
+        own_update[rows, columns] = expanded.astype(BF16)
+
     for copy in started:
         copy.wait_send()
-    for copy in forwards:
-        copy.wait_recv()
+    for half in HALVES:
+        forwards[half].wait_recv()
+        order(1 - c, half, other)
+
+
+def column_tiles(depth, core):
+    for h in range(2):
+        for i in range(depth // ROW_TILE):
+            rows = pl.ds(i * ROW_TILE, ROW_TILE)
+            yield rows, pl.ds(h * 256, 256), pl.ds(pl.multiple_of(h * 512 + core * 256, 256), 256)
 
 
 def reduce_and_gather(*operands):
@@ -254,15 +283,19 @@
     return pl.pallas_call(
         reduce_kernel,
         out_shape=(
-            pltpu.VMEM((2, 2, 2, 2, 2, 2, 2, 2, 16, 128), BF16),
+            pltpu.VMEM((512, 512), BF16),
+            pltpu.VMEM((proj.shape[0], 512), F32),
+            pltpu.VMEM((proj.shape[0], 512), BF16),
             pltpu.VMEM(proj.shape, BF16),
             pltpu.VMEM(weight.shape, F32),
             pltpu.VMEM((16, 256), F32),
             pltpu.VMEM((16, 256), F32),
         ),
         in_specs=[hbm] * 6,
-        out_specs=(vmem,) * 5,
+        out_specs=(vmem,) * 7,
         scratch_shapes=[
+            pltpu.VMEM((2, 2, 2, 2, 2, 2, 2, 2, 16, 128), BF16),
+            pltpu.VMEM((512, 512), BF16),
             pltpu.VMEM((512, 2048), BF16),
             pltpu.VMEM((2, 512, 256), BF16),
             pltpu.VMEM((TOKEN_BLOCKS, 512, 512 // TOKEN_BLOCKS), BF16),
@@ -289,7 +322,9 @@
 
 
 def expand_kernel(
-    gathered,
+    other,
+    own_new,
+    own_update,
     proj,
     weight,
     first_in,
@@ -298,58 +333,39 @@
     update,
     first_out,
     second_out,
-    ordered,
     new_v,
     update_v,
     sems,
     state_sems,
 ):
-    states = [
+    c = lax.axis_index("mp") % 2
+    copies = [
         pltpu.make_async_copy(first_in, first_out, state_sems.at[0]),
         pltpu.make_async_copy(second_in, second_out, state_sems.at[1]),
     ]
-    for copy in states:
+    for copy in copies:
         copy.start()
 
-    def stores(i):
-        rows = pl.ds(i * ROW_TILE, ROW_TILE)
-        return (
-            pltpu.make_async_copy(new_v.at[rows], new_weight.at[rows], sems.at[0, i]),
-            pltpu.make_async_copy(update_v.at[rows], update.at[rows], sems.at[1, i]),
-        )
-
-    for zh in range(2):
-        for c in range(2):
-            for half in range(2):
-                column = zh * 512 + c * 256 + half * 128
-                for x in range(4):
-                    for y in range(4):
-                        for zl in range(2):
-                            at = [place(w, v) for w, v in zip(WRAP_FIRST[half], (x, y, zh * 2 + zl))]
-                            index = tuple(p[0] for p in at) + tuple(p[1] for p in at)
-                            row = x * 128 + y * 32 + zl * 16
-                            ordered[row : row + 16, column : column + 128] = gathered[(c, half, *index)]
-
-    tiles = weight.shape[0] // ROW_TILE
-    for i in range(tiles):
-        rows = pl.ds(i * ROW_TILE, ROW_TILE)
-        left = proj[rows, :]
-        for n in range(4):
-            columns = slice(n * 256, (n + 1) * 256)
-            expanded = jnp.dot(left, ordered[:, columns], preferred_element_type=F32)
-            new_v[rows, columns] = weight[rows, columns] - step_rate * expanded
-            update_v[rows, columns] = expanded.astype(BF16)
-        for copy in stores(i):
+    def store(new, upd, core, i, rows, columns, here):
+        for n, (src, dst) in enumerate(((new, new_weight), (upd, update))):
+            copy = pltpu.make_async_copy(src.at[rows, columns], dst.at[rows, here], sems.at[core, n, i])
             copy.start()
-    for i in range(tiles):
-        for copy in stores(i):
-            copy.wait()
-    for copy in states:
+            copies.append(copy)
+
+    depth = weight.shape[0]
+    for i, at in enumerate(column_tiles(depth, c)):
+        store(own_new, own_update, 0, i, *at)
+    for i, (rows, columns, here) in enumerate(column_tiles(depth, 1 - c)):
+        expanded = jnp.dot(proj[rows, :], other[:, columns], preferred_element_type=F32)
+        new_v[rows, columns] = weight[rows, here] - step_rate * expanded
+        update_v[rows, columns] = expanded.astype(BF16)
+        store(new_v, update_v, 1, i, rows, columns, here)
+    for copy in copies:
         copy.wait()
 
 
-def expand(gathered, proj, weight, first_new, second_new):
-    depth, rank = proj.shape
+def expand(*operands):
+    depth = operands[3].shape[0]
     vmem = pl.BlockSpec(memory_space=pltpu.VMEM)
     hbm = pl.BlockSpec(memory_space=pltpu.HBM)
     return pl.pallas_call(
@@ -360,24 +376,22 @@
             jax.ShapeDtypeStruct((16, 256), F32),
             jax.ShapeDtypeStruct((16, 256), F32),
         ),
-        in_specs=[vmem] * 5,
+        in_specs=[vmem] * 7,
         out_specs=(hbm,) * 4,
         scratch_shapes=[
-            pltpu.VMEM((rank, 1024), BF16),
-            pltpu.VMEM((depth, 1024), F32),
-            pltpu.VMEM((depth, 1024), BF16),
-            pltpu.SemaphoreType.DMA((2, depth // ROW_TILE)),
+            pltpu.VMEM((depth, 512), F32),
+            pltpu.VMEM((depth, 512), BF16),
+            pltpu.SemaphoreType.DMA((2, 2, 2 * depth // ROW_TILE)),
             pltpu.SemaphoreType.DMA((2,)),
         ],
         compiler_params=pltpu.CompilerParams(vmem_limit_bytes=20 * 1024 * 1024),
-    )(gathered, proj, weight, first_new, second_new)
+    )(*operands)
 
 
 def local(activations, out_grads, projector, weight, first_moment, second_moment):
-    gathered, projector, weight, first_new, second_new = reduce_and_gather(
-        activations, out_grads, projector, weight, first_moment, second_moment
+    return tuple(
+        expand(*reduce_and_gather(activations, out_grads, projector, weight, first_moment, second_moment))
     )
-    return tuple(expand(gathered, projector, weight, first_new, second_new))
 
 
 def solution(mesh):

time: 36.7 us -> 36.3 us (0.989)
    pallas_call x1, Pallas kernels: 5.23 us -> 4.86 us  [expand(): pl.pallas_call(expand_kernel, out_shape=(jax.ShapeDtypeStruct((depth, 102...]
where the time goes in v8:
time: 36.3 us; the launch traced here: 36.2 us
  Pallas kernels  35.6 us (98%)
  between operations  0.64 us (2%)
    pallas_call x1, Pallas kernels, reduce_and_gather(): pl.pallas_call(reduce_kernel, out_shape=(pltpu.VMEM((512, 512), BF16), pl...  30.7 us
    pallas_call x1, Pallas kernels, expand(): pl.pallas_call(expand_kernel, out_shape=(jax.ShapeDtypeStruct((depth, 102...  4.86 us

profile of v8, /device:TPU:1, one launch (start us, length us, event | category | flops | bytes accessed | tf_op | source)
XLA Modules:
  0.0 36.2 jit_solution(18135182432437684070)
XLA Ops:
  0.6 30.7 %shard_map.93 = (bf16[512,512]{1,0:T(8,128)(2,1)S(1)}, f32[2048,512]{1,0:T(8,128)S(1)}, bf16[2048,512]{1,0:T(8,128)(2,1)S(1)}, bf16[2048,512]{1,0:T(8,128)(2,1)S...) custom-call(bf16[512,2048]{1,0:T(8,128)(2,1)} %acts.1, bf16[512,1024]{1,0:T(8,128)(2,1)} %grads.1, ...), custom_call_target="tpu_custom_call" | custom-call | tf_op jit(solution)/shard_map/pallas_call | solution.py:283
  31.4 4.9 %shard_map.94 = (f32[2048,1024]{1,0:T(8,128)}, bf16[2048,1024]{1,0:T(8,128)(2,1)}, f32[16,256]{1,0:T(8,128)}, f32[16,256]{1,0:T(8,128)}) custom-call(bf16[512,512]{1,0:T(8,128)(2,1)S(1)} %get-tuple-element.11.other, f32[2048,512]{1,0:T(8,128)S(1)} %get-tuple-element.12.own_new, bf16[2048,512]{1,0:T(8,128)(2,1)S(1)} %get-tuple-element.13.own_update, ...), custom_call_target="tpu_custom_call" | custom-call | tf_op jit(solution)/shard_map/pallas_call | solution.py:371

commit v9 on v8

--- a/solution.py
+++ b/solution.py
@@ -18,12 +18,13 @@
 F32 = jnp.float32
 BF16 = jnp.bfloat16
 TOKEN_BLOCKS = 4
-DEPTH_PARTS = 8
+DEPTH_PARTS = 4
 ROW_TILE = 512
 
 
 WRAP_FIRST = ((False, False, True), (True, True, False))
 HALVES = (1, 0)
+PIECES = ((0, 1), (0, 0), (1, 1), (1, 0))
 
 
 def place(wrap_first, v):
@@ -64,6 +65,7 @@
     sums,
     moments,
     states,
+    seven,
     load_sem,
     pair_send,
     pair_recv,
@@ -152,14 +154,25 @@
         started.append(copy)
         return copy
 
-    def spread(stage, half, flips, source, target=None):
-        copies = []
+    groups = []
+
+    def spread(stage, piece, half, flips, source, target=None):
+        at = (stage, piece, half)
+        groups.append(at)
         for n, m in enumerate(MASKS):
             src = source(m)
             dst = src if target is None else target(n)
-            device = partner(half, flips, m)
-            copies.append(send(src, dst, send_sem.at[stage, half, n], recv_sem.at[stage, half, n], device))
-        return copies
+            pltpu.make_async_remote_copy(
+                src_ref=src,
+                dst_ref=dst,
+                send_sem=send_sem.at[at],
+                recv_sem=recv_sem.at[at],
+                device_id=partner(half, flips, m),
+                device_id_type=MESH,
+            ).start()
+
+    def arrived(stage, piece, half):
+        pltpu.make_async_copy(seven, seven, recv_sem.at[stage, piece, half]).wait()
 
     for k in range(DEPTH_PARTS):
         at = pl.ds(k * depth, depth)
@@ -181,7 +194,16 @@
         pair[t].wait_recv()
         both[:, t * block : (t + 1) * block] = (summed[t] + theirs[t].astype(F32)).astype(BF16)
 
-    stage1, stage2, gather2 = {}, {}, {}
+    def scatter(piece, half):
+        spread(
+            1,
+            piece,
+            half,
+            1,
+            lambda m: parts.at[(half, *flip(sets[half], m), piece)],
+            lambda n: got1.at[half, piece, n],
+        )
+
     for half in HALVES:
         product = jnp.dot(both[...], grads_v[half], preferred_element_type=F32).astype(BF16)
         for x in range(4):
@@ -191,58 +213,53 @@
                     at = [place(w, v) for w, v in zip(WRAP_FIRST[half], (x, y, z))]
                     index = tuple(p[0] for p in at) + tuple(p[1] for p in at)
                     parts[(half, *index)] = product[row : row + 16, column : column + 128]
-        stage1[half] = spread(
-            1, half, 1, lambda m: parts.at[(half, *flip(sets[half], m))], lambda n: got1.at[half, n]
-        )
+        scatter(0, half)
+    for half in HALVES:
+        scatter(1, half)
 
     for copy in load_moments:
         copy.wait()
-    gather0 = {}
-    for half in HALVES:
-        gather0[half] = spread(0, half, 2, lambda m: moments.at[(half, *members[half])])
-
-    for half in HALVES:
-        for copy in stage1[half]:
-            copy.wait_recv()
-        total = parts[(half, *sets[half])].astype(F32)
+    for half in HALVES:
+        spread(0, 0, half, 2, lambda m: moments.at[(half, *members[half])])
+
+    for piece, half in PIECES:
+        arrived(1, piece, half)
+        total = parts[(half, *sets[half], piece)].astype(F32)
         for n in range(7):
-            total += got1[half, n].astype(F32)
-        here = (half, *members[half])
+            total += got1[half, piece, n].astype(F32)
+        here = (half, *members[half], piece)
         sums[here] = total.astype(BF16)
-        stage2[half] = spread(2, half, 2, lambda m: sums.at[here])
-
-    for half in HALVES:
-        for copy in gather0[half]:
-            copy.wait_recv()
-        for copy in stage2[half]:
-            copy.wait_recv()
-        for i in range(2):
-            for j in range(2):
-                for k in range(2):
-                    coefficients = sums[half, 0, 0, 0, i, j, k].astype(F32)
-                    for n in range(1, 8):
-                        coefficients += sums[(half, *bits(n), i, j, k)].astype(F32)
-                    first_new = first_decay * moments[half, i, j, k, 0] + (1.0 - first_decay) * coefficients
-                    second_new = (
-                        second_decay * moments[half, i, j, k, 1]
-                        + (1.0 - second_decay) * coefficients * coefficients
-                    )
-                    normalized = first_new / first_bias / (jnp.sqrt(second_new / second_bias) + epsilon)
-                    gathered[(c, half, *sets[half], i, j, k)] = normalized.astype(BF16)
-                    states[half, i, j, k, 0] = first_new
-                    states[half, i, j, k, 1] = second_new
-        gather2[half] = spread(3, half, 1, lambda m: gathered.at[(c, half, *sets[half])])
+        spread(2, piece, half, 2, lambda m: sums.at[here])
+
+    for half in HALVES:
+        arrived(0, 0, half)
+    for piece, half in PIECES:
+        arrived(2, piece, half)
+        for j in range(2):
+            for k in range(2):
+                coefficients = sums[half, 0, 0, 0, piece, j, k].astype(F32)
+                for n in range(1, 8):
+                    coefficients += sums[(half, *bits(n), piece, j, k)].astype(F32)
+                first_new = first_decay * moments[half, piece, j, k, 0] + (1.0 - first_decay) * coefficients
+                second_new = (
+                    second_decay * moments[half, piece, j, k, 1]
+                    + (1.0 - second_decay) * coefficients * coefficients
+                )
+                normalized = first_new / first_bias / (jnp.sqrt(second_new / second_bias) + epsilon)
+                gathered[(c, half, *sets[half], piece, j, k)] = normalized.astype(BF16)
+                states[half, piece, j, k, 0] = first_new
+                states[half, piece, j, k, 1] = second_new
+        spread(3, piece, half, 1, lambda m: gathered.at[(c, half, *sets[half], piece)])
     for half in range(2):
         columns = slice(half * 128, (half + 1) * 128)
         first_new_ref[:, columns] = states[(half, *members[half], 0)]
         second_new_ref[:, columns] = states[(half, *members[half], 1)]
 
-    forwards = {}
-    for half in HALVES:
-        for copy in gather2[half]:
-            copy.wait_recv()
-        block = gathered.at[c, half]
-        forwards[half] = send(block, block, fw_send.at[half], fw_recv.at[half], sibling)
+    forwards = []
+    for piece, half in PIECES:
+        arrived(3, piece, half)
+        block = gathered.at[c, half, :, :, :, piece]
+        forwards.append(send(block, block, fw_send.at[piece, half], fw_recv.at[piece, half], sibling))
 
     def order(core, half, target):
         for x in range(4):
@@ -261,10 +278,13 @@
         own_new[rows, columns] = weight_v[rows, here] - step_rate * expanded
         own_update[rows, columns] = expanded.astype(BF16)
 
+    for at in groups:
+        pltpu.make_async_copy(seven, seven, send_sem.at[at]).wait()
     for copy in started:
         copy.wait_send()
-    for half in HALVES:
-        forwards[half].wait_recv()
+    for copy in forwards:
+        copy.wait_recv()
+    for half in HALVES:
         order(1 - c, half, other)
 
 
@@ -303,17 +323,18 @@
             pltpu.VMEM((512, 512), BF16),
             pltpu.VMEM((TOKEN_BLOCKS, 512, 512 // TOKEN_BLOCKS), F32),
             pltpu.VMEM((2, 2, 2, 2, 2, 2, 2, 16, 128), BF16),
-            pltpu.VMEM((2, 7, 2, 2, 2, 16, 128), BF16),
+            pltpu.VMEM((2, 2, 7, 2, 2, 16, 128), BF16),
             pltpu.VMEM((2, 2, 2, 2, 2, 2, 2, 16, 128), BF16),
             pltpu.VMEM((2, 2, 2, 2, 2, 16, 128), F32),
             pltpu.VMEM((2, 2, 2, 2, 2, 16, 128), F32),
+            pltpu.VMEM((7, 2, 2, 16, 128), BF16),
             dma((9 + 2 * DEPTH_PARTS,)),
             dma((TOKEN_BLOCKS,)),
             dma((TOKEN_BLOCKS,)),
-            dma((4, 2, 7)),
-            dma((4, 2, 7)),
-            dma((2,)),
-            dma((2,)),
+            dma((4, 2, 2)),
+            dma((4, 2, 2)),
+            dma((2, 2)),
+            dma((2, 2)),
         ],
         compiler_params=pltpu.CompilerParams(
             collective_id=0, has_side_effects=True, vmem_limit_bytes=24 * 1024 * 1024

time: 36.3 us -> 34.1 us (0.939)
  Pallas kernels: 35.6 us -> 33.3 us
    pallas_call x1, Pallas kernels: 30.7 us -> 28.4 us  [reduce_and_gather(): pl.pallas_call(reduce_kernel, out_shape=(pltpu.VMEM((512, 512), BF16), pl...]
where the time goes in v9:
time: 34.1 us; the launch traced here: 33.9 us
  Pallas kernels  33.3 us (98%)
  between operations  0.64 us (2%)
    pallas_call x1, Pallas kernels, reduce_and_gather(): pl.pallas_call(reduce_kernel, out_shape=(pltpu.VMEM((512, 512), BF16), pl...  28.4 us
    pallas_call x1, Pallas kernels, expand(): pl.pallas_call(expand_kernel, out_shape=(jax.ShapeDtypeStruct((depth, 102...  4.86 us

profile of v9, /device:TPU:1, one launch (start us, length us, event | category | flops | bytes accessed | tf_op | source)
XLA Modules:
  0.0 33.9 jit_solution(11303558628337890919)
XLA Ops:
  0.6 28.4 %shard_map.93 = (bf16[512,512]{1,0:T(8,128)(2,1)S(1)}, f32[2048,512]{1,0:T(8,128)S(1)}, bf16[2048,512]{1,0:T(8,128)(2,1)S(1)}, bf16[2048,512]{1,0:T(8,128)(2,1)S...) custom-call(bf16[512,2048]{1,0:T(8,128)(2,1)} %acts.1, bf16[512,1024]{1,0:T(8,128)(2,1)} %grads.1, ...), custom_call_target="tpu_custom_call" | custom-call | tf_op jit(solution)/shard_map/pallas_call | solution.py:303
  29.1 4.9 %shard_map.94 = (f32[2048,1024]{1,0:T(8,128)}, bf16[2048,1024]{1,0:T(8,128)(2,1)}, f32[16,256]{1,0:T(8,128)}, f32[16,256]{1,0:T(8,128)}) custom-call(bf16[512,512]{1,0:T(8,128)(2,1)S(1)} %get-tuple-element.11.other, f32[2048,512]{1,0:T(8,128)S(1)} %get-tuple-element.12.own_new, bf16[2048,512]{1,0:T(8,128)(2,1)S(1)} %get-tuple-element.13.own_update, ...), custom_call_target="tpu_custom_call" | custom-call | tf_op jit(solution)/shard_map/pallas_call | solution.py:392

commit v10 on v9

--- a/solution.py
+++ b/solution.py
@@ -18,7 +18,8 @@
 F32 = jnp.float32
 BF16 = jnp.bfloat16
 TOKEN_BLOCKS = 4
-DEPTH_PARTS = 4
+DEPTHS = (768, 512, 512, 256)
+EARLY_TILES = 2
 ROW_TILE = 512
 
 
@@ -45,6 +46,7 @@
     weight,
     first_moment,
     second_moment,
+    own,
     other,
     own_new,
     own_update,
@@ -53,7 +55,6 @@
     first_new_ref,
     second_new_ref,
     gathered,
-    own,
     acts_v,
     grads_v,
     mine,
@@ -104,11 +105,13 @@
         sets.append(tuple(p[0] for p in places))
         members.append(tuple(p[1] for p in places))
 
-    depth = proj.shape[0] // DEPTH_PARTS
     load_parts = []
 
+    def depth_part(k):
+        return pl.ds(sum(DEPTHS[:k]), DEPTHS[k])
+
     def load_part(k):
-        at = pl.ds(k * depth, depth)
+        at = depth_part(k)
         for n, (src, dst) in enumerate(((proj.at[at], proj_v.at[at]), (acts.at[:, at], acts_v.at[:, at]))):
             copy = pltpu.make_async_copy(src, dst, load_sem.at[2 * k + n])
             copy.start()
@@ -118,7 +121,7 @@
     barrier = pltpu.get_barrier_semaphore()
     for device in [sibling] + [partner(0, flips, m) for flips in (1, 2) for m in MASKS]:
         pl.semaphore_signal(barrier, inc=1, device_id=device, device_id_type=MESH)
-    for k in range(1, DEPTH_PARTS):
+    for k in range(1, len(DEPTHS)):
         load_part(k)
     load_grads = []
     for half in range(2):
@@ -127,7 +130,7 @@
             copy = pltpu.make_async_copy(
                 grads.at[:, columns],
                 grads_v.at[half, :, pl.ds(h * 128, 128)],
-                load_sem.at[2 * DEPTH_PARTS + 2 * half + h],
+                load_sem.at[2 * len(DEPTHS) + 2 * half + h],
             )
             copy.start()
             load_grads.append(copy)
@@ -138,11 +141,11 @@
             copy = pltpu.make_async_copy(
                 moment.at[:, columns],
                 moments.at[(half, *members[half], n)],
-                load_sem.at[4 + 2 * DEPTH_PARTS + 2 * half + n],
+                load_sem.at[4 + 2 * len(DEPTHS) + 2 * half + n],
             )
             copy.start()
             load_moments.append(copy)
-    load_weight = pltpu.make_async_copy(weight, weight_v, load_sem.at[8 + 2 * DEPTH_PARTS])
+    load_weight = pltpu.make_async_copy(weight, weight_v, load_sem.at[8 + 2 * len(DEPTHS)])
 
     started = []
 
@@ -174,8 +177,8 @@
     def arrived(stage, piece, half):
         pltpu.make_async_copy(seven, seven, recv_sem.at[stage, piece, half]).wait()
 
-    for k in range(DEPTH_PARTS):
-        at = pl.ds(k * depth, depth)
+    for k in range(len(DEPTHS)):
+        at = depth_part(k)
         load_parts[2 * k].wait()
         load_parts[2 * k + 1].wait()
         product = jnp.dot(acts_v[:, at], proj_v[at, :], preferred_element_type=F32)
@@ -204,18 +207,18 @@
             lambda n: got1.at[half, piece, n],
         )
 
-    for half in HALVES:
-        product = jnp.dot(both[...], grads_v[half], preferred_element_type=F32).astype(BF16)
-        for x in range(4):
+    for piece, half in PIECES:
+        blocks = [x for x in range(4) if place(WRAP_FIRST[half][0], x)[1] == piece]
+        left = jnp.concatenate([both[x * 128 : (x + 1) * 128, :] for x in blocks], axis=0)
+        product = jnp.dot(left, grads_v[half], preferred_element_type=F32).astype(BF16)
+        for i, x in enumerate(blocks):
             for y in range(4):
                 for z in range(4):
-                    row, column = x * 128 + y * 32 + z % 2 * 16, z // 2 * 128
+                    row, column = i * 128 + y * 32 + z % 2 * 16, z // 2 * 128
                     at = [place(w, v) for w, v in zip(WRAP_FIRST[half], (x, y, z))]
                     index = tuple(p[0] for p in at) + tuple(p[1] for p in at)
                     parts[(half, *index)] = product[row : row + 16, column : column + 128]
-        scatter(0, half)
-    for half in HALVES:
-        scatter(1, half)
+        scatter(piece, half)
 
     for copy in load_moments:
         copy.wait()
@@ -273,10 +276,11 @@
     for half in HALVES:
         order(c, half, own)
     load_weight.wait()
-    for rows, columns, here in column_tiles(weight_v.shape[0], c):
-        expanded = jnp.dot(proj_v[rows, :], own[:, columns], preferred_element_type=F32)
-        own_new[rows, columns] = weight_v[rows, here] - step_rate * expanded
-        own_update[rows, columns] = expanded.astype(BF16)
+    for i, (rows, columns, here) in enumerate(column_tiles(weight_v.shape[0], c)):
+        if i < EARLY_TILES:
+            expanded = jnp.dot(proj_v[rows, :], own[:, columns], preferred_element_type=F32)
+            own_new[i] = weight_v[rows, here] - step_rate * expanded
+            own_update[i] = expanded.astype(BF16)
 
     for at in groups:
         pltpu.make_async_copy(seven, seven, send_sem.at[at]).wait()
@@ -304,18 +308,18 @@
         reduce_kernel,
         out_shape=(
             pltpu.VMEM((512, 512), BF16),
-            pltpu.VMEM((proj.shape[0], 512), F32),
-            pltpu.VMEM((proj.shape[0], 512), BF16),
+            pltpu.VMEM((512, 512), BF16),
+            pltpu.VMEM((EARLY_TILES, ROW_TILE, 256), F32),
+            pltpu.VMEM((EARLY_TILES, ROW_TILE, 256), BF16),
             pltpu.VMEM(proj.shape, BF16),
             pltpu.VMEM(weight.shape, F32),
             pltpu.VMEM((16, 256), F32),
             pltpu.VMEM((16, 256), F32),
         ),
         in_specs=[hbm] * 6,
-        out_specs=(vmem,) * 7,
+        out_specs=(vmem,) * 8,
         scratch_shapes=[
             pltpu.VMEM((2, 2, 2, 2, 2, 2, 2, 2, 16, 128), BF16),
-            pltpu.VMEM((512, 512), BF16),
             pltpu.VMEM((512, 2048), BF16),
             pltpu.VMEM((2, 512, 256), BF16),
             pltpu.VMEM((TOKEN_BLOCKS, 512, 512 // TOKEN_BLOCKS), BF16),
@@ -328,7 +332,7 @@
             pltpu.VMEM((2, 2, 2, 2, 2, 16, 128), F32),
             pltpu.VMEM((2, 2, 2, 2, 2, 16, 128), F32),
             pltpu.VMEM((7, 2, 2, 16, 128), BF16),
-            dma((9 + 2 * DEPTH_PARTS,)),
+            dma((9 + 2 * len(DEPTHS),)),
             dma((TOKEN_BLOCKS,)),
             dma((TOKEN_BLOCKS,)),
             dma((4, 2, 2)),
@@ -343,6 +347,7 @@
 
 
 def expand_kernel(
+    own,
     other,
     own_new,
     own_update,
@@ -367,26 +372,29 @@
     for copy in copies:
         copy.start()
 
-    def store(new, upd, core, i, rows, columns, here):
+    def store(new, upd, core, i, rows, here):
         for n, (src, dst) in enumerate(((new, new_weight), (upd, update))):
-            copy = pltpu.make_async_copy(src.at[rows, columns], dst.at[rows, here], sems.at[core, n, i])
+            copy = pltpu.make_async_copy(src.at[i], dst.at[rows, here], sems.at[core, n, i])
             copy.start()
             copies.append(copy)
 
     depth = weight.shape[0]
-    for i, at in enumerate(column_tiles(depth, c)):
-        store(own_new, own_update, 0, i, *at)
-    for i, (rows, columns, here) in enumerate(column_tiles(depth, 1 - c)):
-        expanded = jnp.dot(proj[rows, :], other[:, columns], preferred_element_type=F32)
-        new_v[rows, columns] = weight[rows, here] - step_rate * expanded
-        update_v[rows, columns] = expanded.astype(BF16)
-        store(new_v, update_v, 1, i, rows, columns, here)
+    for core, normalized in ((0, own), (1, other)):
+        for i, (rows, columns, here) in enumerate(column_tiles(depth, c if core == 0 else 1 - c)):
+            if core == 0 and i < EARLY_TILES:
+                store(own_new, own_update, core, i, rows, here)
+                continue
+            expanded = jnp.dot(proj[rows, :], normalized[:, columns], preferred_element_type=F32)
+            new_v[core, i] = weight[rows, here] - step_rate * expanded
+            update_v[core, i] = expanded.astype(BF16)
+            store(new_v.at[core], update_v.at[core], core, i, rows, here)
     for copy in copies:
         copy.wait()
 
 
 def expand(*operands):
-    depth = operands[3].shape[0]
+    depth = operands[4].shape[0]
+    tiles = 2 * depth // ROW_TILE
     vmem = pl.BlockSpec(memory_space=pltpu.VMEM)
     hbm = pl.BlockSpec(memory_space=pltpu.HBM)
     return pl.pallas_call(
@@ -397,12 +405,12 @@
             jax.ShapeDtypeStruct((16, 256), F32),
             jax.ShapeDtypeStruct((16, 256), F32),
         ),
-        in_specs=[vmem] * 7,
+        in_specs=[vmem] * 8,
         out_specs=(hbm,) * 4,
         scratch_shapes=[
-            pltpu.VMEM((depth, 512), F32),
-            pltpu.VMEM((depth, 512), BF16),
-            pltpu.SemaphoreType.DMA((2, 2, 2 * depth // ROW_TILE)),
+            pltpu.VMEM((2, tiles, ROW_TILE, 256), F32),
+            pltpu.VMEM((2, tiles, ROW_TILE, 256), BF16),
+            pltpu.SemaphoreType.DMA((2, 2, tiles)),
             pltpu.SemaphoreType.DMA((2,)),
         ],
         compiler_params=pltpu.CompilerParams(vmem_limit_bytes=20 * 1024 * 1024),

time: 34.1 us -> 34 us (level)
  no operation moved by 1% of the time
where the time goes in v10:
time: 34 us; the launch traced here: 33.8 us
  Pallas kernels  33.2 us (98%)
  between operations  0.64 us (2%)
    pallas_call x1, Pallas kernels, reduce_and_gather(): pl.pallas_call(reduce_kernel, out_shape=(pltpu.VMEM((512, 512), BF16), pl...  28.3 us
    pallas_call x1, Pallas kernels, expand(): pl.pallas_call(expand_kernel, out_shape=(jax.ShapeDtypeStruct((depth, 102...  4.86 us

profile of v10, /device:TPU:1, one launch (start us, length us, event | category | flops | bytes accessed | tf_op | source)
XLA Modules:
  0.0 33.8 jit_solution(10159582741603115331)
XLA Ops:
  0.6 28.3 %shard_map.93 = (bf16[512,512]{1,0:T(8,128)(2,1)S(1)}, bf16[512,512]{1,0:T(8,128)(2,1)S(1)}, f32[2,512,256]{2,1,0:T(8,128)S(1)}, bf16[2,512,256]{2,1,0:T(8,128)(...) custom-call(bf16[512,2048]{1,0:T(8,128)(2,1)} %acts.1, ...), custom_call_target="tpu_custom_call" | custom-call | tf_op jit(solution)/shard_map/pallas_call | solution.py:307
  29.0 4.9 %shard_map.94 = (f32[2048,1024]{1,0:T(8,128)}, bf16[2048,1024]{1,0:T(8,128)(2,1)}, f32[16,256]{1,0:T(8,128)}, f32[16,256]{1,0:T(8,128)}) custom-call(bf16[512,512]{1,0:T(8,128)(2,1)S(1)} %get-tuple-element.12.own, bf16[512,512]{1,0:T(8,128)(2,1)S(1)} %get-tuple-element.13.other, f32[2,512,256]{2,1,0:T(8,128)S(1)} %get-tuple-element.14.own_new, ...), custom_call_target="tpu_custom_call" | custom-call | tf_op jit(solution)/shard_map/pallas_call | solution.py:400

commit v11 on v10

--- a/solution.py
+++ b/solution.py
@@ -26,6 +26,7 @@
 WRAP_FIRST = ((False, False, True), (True, True, False))
 HALVES = (1, 0)
 PIECES = ((0, 1), (0, 0), (1, 1), (1, 0))
+ARRIVING = ((0, 0), (0, 1), (1, 0), (1, 1))
 
 
 def place(wrap_first, v):
@@ -184,12 +185,14 @@
         product = jnp.dot(acts_v[:, at], proj_v[at, :], preferred_element_type=F32)
         projected = product if k == 0 else projected + product
     block = projected.shape[0] // TOKEN_BLOCKS
+    pair = []
     for t in range(TOKEN_BLOCKS):
         turned = projected[t * block : (t + 1) * block].T
         summed[t] = turned
         mine[t] = turned.astype(BF16)
-    pl.semaphore_wait(barrier, 15)
-    pair = [send(mine.at[t], theirs.at[t], pair_send.at[t], pair_recv.at[t], sibling) for t in range(TOKEN_BLOCKS)]
+        if t == 0:
+            pl.semaphore_wait(barrier, 15)
+        pair.append(send(mine.at[t], theirs.at[t], pair_send.at[t], pair_recv.at[t], sibling))
     for copy in load_grads:
         copy.wait()
     load_weight.start()
@@ -225,7 +228,7 @@
     for half in HALVES:
         spread(0, 0, half, 2, lambda m: moments.at[(half, *members[half])])
 
-    for piece, half in PIECES:
+    for piece, half in ARRIVING:
         arrived(1, piece, half)
         total = parts[(half, *sets[half], piece)].astype(F32)
         for n in range(7):
@@ -259,7 +262,7 @@
         second_new_ref[:, columns] = states[(half, *members[half], 1)]
 
     forwards = []
-    for piece, half in PIECES:
+    for piece, half in ARRIVING:
         arrived(3, piece, half)
         block = gathered.at[c, half, :, :, :, piece]
         forwards.append(send(block, block, fw_send.at[piece, half], fw_recv.at[piece, half], sibling))

time: 34 us -> 33.5 us (0.985)
  Pallas kernels: 33.2 us -> 32.7 us
    pallas_call x1, Pallas kernels: 28.3 us -> 27.9 us  [reduce_and_gather(): pl.pallas_call(reduce_kernel, out_shape=(pltpu.VMEM((512, 512), BF16), pl...]
where the time goes in v11:
time: 33.5 us; the launch traced here: 33.4 us
  Pallas kernels  32.7 us (98%)
  between operations  0.64 us (2%)
    pallas_call x1, Pallas kernels, reduce_and_gather(): pl.pallas_call(reduce_kernel, out_shape=(pltpu.VMEM((512, 512), BF16), pl...  27.9 us
    pallas_call x1, Pallas kernels, expand(): pl.pallas_call(expand_kernel, out_shape=(jax.ShapeDtypeStruct((depth, 102...  4.86 us

profile of v11, /device:TPU:1, one launch (start us, length us, event | category | flops | bytes accessed | tf_op | source)
XLA Modules:
  0.0 33.4 jit_solution(1561229764883571829)
XLA Ops:
  0.6 27.9 %shard_map.93 = (bf16[512,512]{1,0:T(8,128)(2,1)S(1)}, bf16[512,512]{1,0:T(8,128)(2,1)S(1)}, f32[2,512,256]{2,1,0:T(8,128)S(1)}, bf16[2,512,256]{2,1,0:T(8,128)(...) custom-call(bf16[512,2048]{1,0:T(8,128)(2,1)} %acts.1, ...), custom_call_target="tpu_custom_call" | custom-call | tf_op jit(solution)/shard_map/pallas_call | solution.py:310
  28.5 4.9 %shard_map.94 = (f32[2048,1024]{1,0:T(8,128)}, bf16[2048,1024]{1,0:T(8,128)(2,1)}, f32[16,256]{1,0:T(8,128)}, f32[16,256]{1,0:T(8,128)}) custom-call(bf16[512,512]{1,0:T(8,128)(2,1)S(1)} %get-tuple-element.12.own, bf16[512,512]{1,0:T(8,128)(2,1)S(1)} %get-tuple-element.13.other, f32[2,512,256]{2,1,0:T(8,128)S(1)} %get-tuple-element.14.own_new, ...), custom_call_target="tpu_custom_call" | custom-call | tf_op jit(solution)/shard_map/pallas_call | solution.py:403

commit v12 on v11

--- a/solution.py
+++ b/solution.py
@@ -193,6 +193,11 @@
         if t == 0:
             pl.semaphore_wait(barrier, 15)
         pair.append(send(mine.at[t], theirs.at[t], pair_send.at[t], pair_recv.at[t], sibling))
+    for copy in load_moments:
+        copy.wait()
+    for half in HALVES:
+        spread(0, 0, half, 2, lambda m: moments.at[(half, *members[half])])
+
     for copy in load_grads:
         copy.wait()
     load_weight.start()
@@ -222,11 +227,6 @@
                     index = tuple(p[0] for p in at) + tuple(p[1] for p in at)
                     parts[(half, *index)] = product[row : row + 16, column : column + 128]
         scatter(piece, half)
-
-    for copy in load_moments:
-        copy.wait()
-    for half in HALVES:
-        spread(0, 0, half, 2, lambda m: moments.at[(half, *members[half])])
 
     for piece, half in ARRIVING:
         arrived(1, piece, half)
@@ -261,11 +261,11 @@
         first_new_ref[:, columns] = states[(half, *members[half], 0)]
         second_new_ref[:, columns] = states[(half, *members[half], 1)]
 
-    forwards = []
+    forwards = ([], [])
     for piece, half in ARRIVING:
         arrived(3, piece, half)
         block = gathered.at[c, half, :, :, :, piece]
-        forwards.append(send(block, block, fw_send.at[piece, half], fw_recv.at[piece, half], sibling))
+        forwards[half].append(send(block, block, fw_send.at[piece, half], fw_recv.at[piece, half], sibling))
 
     def order(core, half, target):
         for x in range(4):
@@ -289,9 +289,9 @@
         pltpu.make_async_copy(seven, seven, send_sem.at[at]).wait()
     for copy in started:
         copy.wait_send()
-    for copy in forwards:
-        copy.wait_recv()
-    for half in HALVES:
+    for half in range(2):
+        for copy in forwards[half]:
+            copy.wait_recv()
         order(1 - c, half, other)
 
 

time: 33.5 us -> 33.8 us (level)
  no operation moved by 1% of the time
where the time goes in v12:
time: 33.8 us; the launch traced here: 33.7 us
  Pallas kernels  33 us (98%)
  between operations  0.64 us (2%)
    pallas_call x1, Pallas kernels, reduce_and_gather(): pl.pallas_call(reduce_kernel, out_shape=(pltpu.VMEM((512, 512), BF16), pl...  28.2 us
    pallas_call x1, Pallas kernels, expand(): pl.pallas_call(expand_kernel, out_shape=(jax.ShapeDtypeStruct((depth, 102...  4.86 us

profile of v12, /device:TPU:1, one launch (start us, length us, event | category | flops | bytes accessed | tf_op | source)
XLA Modules:
  0.0 33.7 jit_solution(16145916901487111599)
XLA Ops:
  0.6 28.2 %shard_map.93 = (bf16[512,512]{1,0:T(8,128)(2,1)S(1)}, bf16[512,512]{1,0:T(8,128)(2,1)S(1)}, f32[2,512,256]{2,1,0:T(8,128)S(1)}, bf16[2,512,256]{2,1,0:T(8,128)(...) custom-call(bf16[512,2048]{1,0:T(8,128)(2,1)} %acts.1, ...), custom_call_target="tpu_custom_call" | custom-call | tf_op jit(solution)/shard_map/pallas_call | solution.py:310
  28.8 4.9 %shard_map.94 = (f32[2048,1024]{1,0:T(8,128)}, bf16[2048,1024]{1,0:T(8,128)(2,1)}, f32[16,256]{1,0:T(8,128)}, f32[16,256]{1,0:T(8,128)}) custom-call(bf16[512,512]{1,0:T(8,128)(2,1)S(1)} %get-tuple-element.12.own, bf16[512,512]{1,0:T(8,128)(2,1)S(1)} %get-tuple-element.13.other, f32[2,512,256]{2,1,0:T(8,128)S(1)} %get-tuple-element.14.own_new, ...), custom_call_target="tpu_custom_call" | custom-call | tf_op jit(solution)/shard_map/pallas_call | solution.py:403

commit v13 on v12

--- a/solution.py
+++ b/solution.py
@@ -200,7 +200,6 @@
 
     for copy in load_grads:
         copy.wait()
-    load_weight.start()
     for t in range(TOKEN_BLOCKS):
         pair[t].wait_recv()
         both[:, t * block : (t + 1) * block] = (summed[t] + theirs[t].astype(F32)).astype(BF16)
@@ -227,6 +226,7 @@
                     index = tuple(p[0] for p in at) + tuple(p[1] for p in at)
                     parts[(half, *index)] = product[row : row + 16, column : column + 128]
         scatter(piece, half)
+    load_weight.start()
 
     for piece, half in ARRIVING:
         arrived(1, piece, half)

time: 33.8 us -> 33.8 us (level)
  no operation moved by 1% of the time
where the time goes in v13:
time: 33.8 us; the launch traced here: 33.7 us
  Pallas kernels  33 us (98%)
  between operations  0.64 us (2%)
    pallas_call x1, Pallas kernels, reduce_and_gather(): pl.pallas_call(reduce_kernel, out_shape=(pltpu.VMEM((512, 512), BF16), pl...  28.2 us
    pallas_call x1, Pallas kernels, expand(): pl.pallas_call(expand_kernel, out_shape=(jax.ShapeDtypeStruct((depth, 102...  4.86 us

profile of v13, /device:TPU:1, one launch (start us, length us, event | category | flops | bytes accessed | tf_op | source)
XLA Modules:
  0.0 33.7 jit_solution(2082769990404836065)
XLA Ops:
  0.6 28.2 %shard_map.93 = (bf16[512,512]{1,0:T(8,128)(2,1)S(1)}, bf16[512,512]{1,0:T(8,128)(2,1)S(1)}, f32[2,512,256]{2,1,0:T(8,128)S(1)}, bf16[2,512,256]{2,1,0:T(8,128)(...) custom-call(bf16[512,2048]{1,0:T(8,128)(2,1)} %acts.1, ...), custom_call_target="tpu_custom_call" | custom-call | tf_op jit(solution)/shard_map/pallas_call | solution.py:310
  28.8 4.9 %shard_map.94 = (f32[2048,1024]{1,0:T(8,128)}, bf16[2048,1024]{1,0:T(8,128)(2,1)}, f32[16,256]{1,0:T(8,128)}, f32[16,256]{1,0:T(8,128)}) custom-call(bf16[512,512]{1,0:T(8,128)(2,1)S(1)} %get-tuple-element.12.own, bf16[512,512]{1,0:T(8,128)(2,1)S(1)} %get-tuple-element.13.other, f32[2,512,256]{2,1,0:T(8,128)S(1)} %get-tuple-element.14.own_new, ...), custom_call_target="tpu_custom_call" | custom-call | tf_op jit(solution)/shard_map/pallas_call | solution.py:403
